TPU v7x, 512 devices: a whole 4x4x16 slice. The times are simulated.
512 devices in a mesh: gx: 16 (over z_lo, y), gy: 32 (over x, z_hi, core).
Axes of the slice: x: 4, y: 4, z: 16 (z_hi: 4, z_lo: 4; z = z_hi * 4 + z_lo), core: 2. Of those that a mesh axis runs over, the one named last changes fastest.
Arguments:
- a_blocks: bfloat16 [64, 64, 5, 192, 192], P('gx', 'gy'), may hold values from -0.4375 to 0.4375
- a_codes: int32 [64, 64, 5], P('gx', 'gy'), may hold values from 0 to 9, as said below
- p_blocks: bfloat16 [64, 64, 3, 12, 192], P('gx', 'gy'), may hold values from -0.875 to 0.875
- p_codes: int32 [64, 64, 3], P('gx', 'gy'), may hold values from 0 to 5, as said below
Outputs:
- coarse: float32 [64, 64, 12, 588], P('gx', 'gy')
Inputs may be any that keep to these rules, and one draw needn't show every extreme that they name: `a_codes`: slot 0 is 4 (the aggregate itself); the other slots of one aggregate hold distinct codes or 9; some aggregates have every slot live. `p_codes`: slot 0 is 0 (the aggregate itself); the other slots of one aggregate hold distinct codes of 1 to 4 or 5; some aggregates have every slot live.
All inputs are finite; a program needn't handle non-finite values.
Results may differ from a plain program's by a relative error of at most 0.0029.
Values may be sent and summed in bfloat16 or wider, within the bound.
A program may use at most 64 MiB of HBM per device.

v0:
```python
import jax
import jax.numpy as jnp
import numpy as np
from jax import lax
from jax.sharding import PartitionSpec as P

near_steps = tuple(((shift_x, shift_y) for shift_x in (-1, 0, 1) for shift_y in (-1, 0, 1)))
face_steps = ((0, 0), (-1, 0), (1, 0), (0, -1), (0, 1))


def extended(cells, sides, width):
    for axis, dim in sides:
        count = lax.axis_size(axis)
        ends = count - 1
        head = lax.slice_in_dim(cells, 0, width, axis=dim)
        tail = lax.slice_in_dim(cells, cells.shape[dim] - width, cells.shape[dim], axis=dim)
        cells = jnp.concatenate(
            [
                lax.ppermute(tail, axis, [(i, (i + 1) % count) for i in range(ends)]),
                cells,
                lax.ppermute(head, axis, [((i + 1) % count, i) for i in range(ends)]),
            ],
            axis=dim,
        )
    return cells


def spread_table():
    table = np.zeros((9, 5, 25), np.float32)
    for near_index, (shift_x, shift_y) in enumerate(near_steps):
        for face_index, (face_x, face_y) in enumerate(face_steps):
            table[near_index, face_index, (shift_x + face_x + 2) * 5 + shift_y + face_y + 2] = 1.0
    return table


def row_products(a_rows, a_slots, near_blocks):
    amount = a_rows.shape[0]
    flat_near = near_blocks.reshape((9 * amount,) + near_blocks.shape[2:])
    spread = jnp.asarray(spread_table()).reshape(9, 125)
    summed = jnp.zeros((amount, 25) + near_blocks.shape[3:], jnp.float32)
    for slot_index in range(a_slots.shape[1]):
        slot_codes = a_slots[:, slot_index]
        picked = jnp.minimum(slot_codes, 8) * amount + jnp.arange(amount, dtype=jnp.int32)
        chosen = flat_near[picked]
        product = jnp.einsum(
            "nqcj,nij->nqci", chosen, a_rows[:, slot_index], preferred_element_type=jnp.float32
        )
        weights = jnp.dot(
            jax.nn.one_hot(slot_codes, 9, dtype=jnp.float32),
            spread,
            precision=lax.Precision.HIGHEST,
        ).reshape(amount, 5, 25)
        summed = summed + jnp.einsum(
            "nqo,nqci->noci", weights, product, precision=lax.Precision.HIGHEST
        )
    return summed.astype(jnp.bfloat16)


def coarse_part(face_rows, coupled, face_index):
    terms = jnp.einsum("nci,noei->ncoe", face_rows, coupled, preferred_element_type=jnp.float32)
    amount, unknowns = (terms.shape[0], terms.shape[1])
    face_x, face_y = face_steps[face_index]
    layout = terms.reshape(amount, unknowns, 5, 5, unknowns)
    layout = jnp.pad(
        layout, ((0, 0), (0, 0), (1 - face_x, 1 + face_x), (1 - face_y, 1 + face_y), (0, 0))
    )
    return layout.reshape(amount, unknowns, 49 * unknowns)


def shards(a_blocks, a_codes, p_blocks, p_codes):
    tile_x, tile_y, slots_a = a_codes.shape
    amount = tile_x * tile_y
    unknowns, edges = (p_blocks.shape[3], p_blocks.shape[4])
    face_blocks = jnp.einsum(
        "xymf,xymcj->xyfcj",
        jax.nn.one_hot(p_codes, 5, dtype=jnp.bfloat16),
        p_blocks,
        preferred_element_type=jnp.float32,
    ).astype(jnp.bfloat16)
    face_cycle = extended(face_blocks, (("gx", 0), ("gy", 1)), 1)
    near_blocks = jnp.stack(
        [
            face_cycle[1 + shift_x : 1 + shift_x + tile_x, 1 + shift_y : 1 + shift_y + tile_y]
            for shift_x, shift_y in near_steps
        ]
    )
    near_blocks = near_blocks.reshape(9, amount, 5, unknowns, edges)
    coupled = row_products(
        a_blocks.reshape(amount, slots_a, edges, edges),
        a_codes.reshape(amount, slots_a),
        near_blocks,
    )
    coupled = coupled.reshape(tile_x, tile_y, 25, unknowns, edges)
    coupled_cycle = extended(coupled, (("gx", 0), ("gy", 1)), 1)
    summed = jnp.zeros((amount, unknowns, 49 * unknowns), jnp.float32)
    for face_index, (face_x, face_y) in enumerate(face_steps):
        face_rows = face_cycle[
            1 - face_x : 1 - face_x + tile_x, 1 - face_y : 1 - face_y + tile_y, face_index
        ]
        coupled_rows = coupled_cycle[
            1 - face_x : 1 - face_x + tile_x, 1 - face_y : 1 - face_y + tile_y
        ]
        summed = summed + coarse_part(
            face_rows.reshape(amount, unknowns, edges),
            coupled_rows.reshape(amount, 25, unknowns, edges),
            face_index,
        )
    return summed.reshape(tile_x, tile_y, unknowns, 49 * unknowns)


def solution(mesh):
    in_specs = (
        P("gx", "gy", None, None, None),
        P("gx", "gy", None),
        P("gx", "gy", None, None, None),
        P("gx", "gy", None),
    )
    out_specs = P("gx", "gy", None, None)
    return jax.shard_map(shards, mesh=mesh, in_specs=in_specs, out_specs=out_specs, check_vma=False)
```

profile of v0, /device:TPU:38, one launch (start us, length us, event | category | flops | bytes accessed | tf_op | source)
XLA Modules:
  0.0 193.9 jit_solution(4560919621217861160)
XLA Ops:
  1.4 3.5 %collective-permute-start = (bf16[1,2,5,12,192]{4,2,3,1,0:T(8,128)(2,1)S(1)}, bf16[1,2,5,12,192]{4,2,3,1,0:T(8,128)(2,1)S(1)}, u32[]{:S(2)}, u32[]{:S(2)}) collective-permute-start(bf16[1,2,5,12,192]{4,2,3,1,0:T(8,128)(2,1)S(1)} %get-tuple-element.32), channel_id=1, source_target_pairs={{0,32},{32,64},{64,96},{96,128},{128,160},{160,192},{192,224},{224... | collective-permute-start | bytes 138248 | tf_op jit(solution)/shard_map/ppermute | solution.py:19
  4.8 4.5 %collective-permute-start.1 = (bf16[1,2,5,12,192]{4,2,3,1,0:T(8,128)(2,1)S(1)}, bf16[1,2,5,12,192]{4,2,3,1,0:T(8,128)(2,1)S(1)}, u32[]{:S(2)}, u32[]{:S(2)}) collective-permute-start(bf16[1,2,5,12,192]{4,2,3,1,0:T(8,128)(2,1)S(1)} %get-tuple-element.33), channel_id=1, source_target_pairs={{32,0},{64,32},{96,64},{128,96},{160,128},{192,160},{224,192},{256... | collective-permute-start | bytes 138248 | tf_op jit(solution)/shard_map/ppermute | solution.py:21
  9.3 1.2 slice_reduce_fusion
  10.5 1.8 convolution_bitcast_fusion
  12.3 1.1 convolution_bitcast_fusion.1
  13.5 1.2 convolution_bitcast_fusion.2
  14.6 1.2 convolution_bitcast_fusion.3
  16.1 11.0 %collective-permute-start.3 = (bf16[6,1,5,12,192]{4,2,3,1,0:T(8,128)(2,1)S(1)}, bf16[6,1,5,12,192]{4,2,3,1,0:T(8,128)(2,1)S(1)}, u32[]{:S(2)}, u32[]{:S(2)}) collective-permute-start(bf16[6,1,5,12,192]{4,2,3,1,0:T(8,128)(2,1)S(1)} %get-tuple-element.27), channel_id=1, source_target_pairs={{1,0},{2,1},{3,2},{4,3},{5,4},{6,5},{7,6},{8,7},{9,8},{10,9},{11,1... | collective-permute-start | bytes 414728 | tf_op jit(solution)/shard_map/ppermute | solution.py:21
  27.1 1.9 collective-permute-start.2
  29.3 8.3 %collective-permute-done.3 = bf16[6,1,5,12,192]{4,2,3,1,0:T(8,128)(2,1)S(1)} collective-permute-done((bf16[6,1,5,12,192]{4,2,3,1,0:T(8,128)(2,1)S(1)}, bf16[6,1,5,12,192]{4,2,3,1,0:T(8,128)(2,1)S(1)}, u32[]{:S(2)}, u32[]{:S(2)}) %collective-permute-start.3) | collective-permute-done | bytes 138272 | tf_op jit(solution)/shard_map/ppermute | solution.py:21
  37.6 3.9 %collective-permute-done.2 = bf16[6,1,5,12,192]{4,2,3,1,0:T(8,128)(2,1)S(1)} collective-permute-done((bf16[6,1,5,12,192]{4,2,3,1,0:T(8,128)(2,1)S(1)}, bf16[6,1,5,12,192]{4,2,3,1,0:T(8,128)(2,1)S(1)}, u32[]{:S(2)}, u32[]{:S(2)}) %collective-permute-start.2) | collective-permute-done | bytes 138272 | tf_op jit(solution)/shard_map/ppermute | solution.py:19
  42.3 1.7 copy-done.7
  44.1 2.6 %gather_fusion.4 = bf16[8,5,12,192]{3,1,2,0:T(8,128)(2,1)S(1)} fusion(bf16[72,5,12,192]{3,1,2,0:T(8,128)(2,1)} %bitcast.159, s32[1024]{0:T(1024)S(1)} %get-tuple-element.34), kind=kCustom, calls=%fused_computation.4 | custom fusion | bytes 368672 | tf_op jit(solution)/shard_map/gather | solution.py:44
  46.7 2.6 %gather_fusion.3 = bf16[8,5,12,192]{3,1,2,0:T(8,128)(2,1)S(1)} fusion(bf16[72,5,12,192]{3,1,2,0:T(8,128)(2,1)} %bitcast.160, s32[1024]{0:T(1024)S(1)} %get-tuple-element.35), kind=kCustom, calls=%fused_computation.3 | custom fusion | bytes 368672 | tf_op jit(solution)/shard_map/gather | solution.py:44
  49.2 1.5 fusion
  50.8 1.5 fusion.1
  52.3 3.3 %gather_fusion.2 = bf16[8,5,12,192]{3,1,2,0:T(8,128)(2,1)} fusion(bf16[72,5,12,192]{3,1,2,0:T(8,128)(2,1)} %bitcast.161, s32[1024]{0:T(1024)S(1)} %get-tuple-element.36), kind=kCustom, calls=%fused_computation.2 | custom fusion | bytes 368672 | tf_op jit(solution)/shard_map/gather | solution.py:44
  55.6 1.6 fusion.2
  57.2 3.3 %gather_fusion.1 = bf16[8,5,12,192]{3,1,2,0:T(8,128)(2,1)} fusion(bf16[72,5,12,192]{3,1,2,0:T(8,128)(2,1)} %bitcast.162, s32[1024]{0:T(1024)S(1)} %get-tuple-element.37), kind=kCustom, calls=%fused_computation.1 | custom fusion | bytes 368672 | tf_op jit(solution)/shard_map/gather | solution.py:44
  60.6 3.3 %gather_fusion = bf16[8,5,12,192]{3,1,2,0:T(8,128)(2,1)} fusion(bf16[72,5,12,192]{3,1,2,0:T(8,128)(2,1)} %bitcast.163, s32[1024]{0:T(1024)S(1)} %pad_clamp_fusion.4), kind=kCustom, calls=%fused_computation | custom fusion | bytes 368672 | tf_op jit(solution)/shard_map/gather | solution.py:44
  63.9 1.6 fusion.4
  65.5 1.6 fusion.3
  67.1 2.9 %fusion.10 = f32[8,25,12,192]{3,1,2,0:T(8,128)S(1)} fusion(f32[8,5,12,192]{3,2,1,0:T(8,128)S(1)} %fusion.3, f32[8,5,25,1]{2,0,1,3:T(8,128)S(1)} %convolution_bitcast_fusion.3), kind=kOutput, calls=%fused_computation.39 | convolution fusion | flops 27648000 | bytes 2215840 | tf_op jit(solution)/shard_map/nqo,nqci->noci/dot_general | solution.py:53
  70.0 2.9 %fusion.12 = f32[8,25,12,192]{3,1,2,0:T(8,128)S(1)} fusion(f32[8,5,12,192]{3,2,1,0:T(8,128)S(1)} %fusion.4, f32[8,5,25,1]{2,0,1,3:T(8,128)S(1)} %convolution_bitcast_fusion.4), kind=kOutput, calls=%fused_computation.41 | convolution fusion | flops 27648000 | bytes 2215840 | tf_op jit(solution)/shard_map/nqo,nqci->noci/dot_general | solution.py:53
  72.9 2.9 %fusion.8 = f32[8,25,12,192]{3,1,2,0:T(8,128)S(1)} fusion(f32[8,5,12,192]{3,2,1,0:T(8,128)S(1)} %fusion.2, f32[8,5,25,1]{2,0,1,3:T(8,128)S(1)} %convolution_bitcast_fusion.2), kind=kOutput, calls=%fused_computation.37 | convolution fusion | flops 27648000 | bytes 2215840 | tf_op jit(solution)/shard_map/nqo,nqci->noci/dot_general | solution.py:53
  75.8 3.1 %fusion.6 = f32[8,25,12,192]{3,1,2,0:T(8,128)S(1)} fusion(f32[8,5,12,192]{3,2,1,0:T(8,128)S(1)} %fusion.1, f32[8,5,25,1]{2,0,1,3:T(8,128)S(1)} %convolution_bitcast_fusion.1), kind=kOutput, calls=%fused_computation.35 | convolution fusion | flops 27648000 | bytes 2215840 | tf_op jit(solution)/shard_map/nqo,nqci->noci/dot_general | solution.py:53
  78.9 3.4 %add_convert_fusion = bf16[8,25,12,192]{3,1,2,0:T(8,128)(2,1)S(1)} fusion(f32[8,25,12,192]{3,1,2,0:T(8,128)S(1)} %fusion.6, f32[8,25,12,192]{3,1,2,0:T(8,128)S(1)} %fusion.8, f32[8,25,12,192]{3,1,2,0:T(8,128)S(1)} %fusion.12, f32[8,25,12,192]{3,1,2,0:T(8,128)S(1)} %fusion.10, f32[8,5,12,192]{3,2,1,0:T(8,128)S(1)} %fusion, f32[8,5,25,1]{2,0,1,3:T(8,128)S(1)} %copy-done.8), kind=kOutput, calls=%fused_computation.5 | convolution fusion | flops 29952000 | bytes 8667040 | tf_op jit(solution)/shard_map/nqo,nqci->noci/dot_general | solution.py:53
  82.3 3.8 %collective-permute-start.5 = (bf16[1,2,25,12,192]{4,2,3,1,0:T(8,128)(2,1)S(1)}, bf16[1,2,25,12,192]{4,2,3,1,0:T(8,128)(2,1)S(1)}, u32[]{:S(2)}, u32[]{:S(2)}) collective-permute-start(bf16[1,2,25,12,192]{4,2,3,1,0:T(8,128)(2,1)S(1)} %get-tuple-element.21), channel_id=1, source_target_pairs={{0,32},{32,64},{64,96},{96,128},{128,160},{160,192},{192,224},{224... | collective-permute-start | bytes 691208 | tf_op jit(solution)/shard_map/ppermute | solution.py:19
  86.2 9.4 %collective-permute-start.4 = (bf16[1,2,25,12,192]{4,2,3,1,0:T(8,128)(2,1)S(1)}, bf16[1,2,25,12,192]{4,2,3,1,0:T(8,128)(2,1)S(1)}, u32[]{:S(2)}, u32[]{:S(2)}) collective-permute-start(bf16[1,2,25,12,192]{4,2,3,1,0:T(8,128)(2,1)S(1)} %get-tuple-element.22), channel_id=1, source_target_pairs={{32,0},{64,32},{96,64},{128,96},{160,128},{192,160},{224,192},{256... | collective-permute-start | bytes 691208 | tf_op jit(solution)/shard_map/ppermute | solution.py:21
  95.6 3.8 %collective-permute-done.5 = bf16[1,2,25,12,192]{4,2,3,1,0:T(8,128)(2,1)S(1)} collective-permute-done((bf16[1,2,25,12,192]{4,2,3,1,0:T(8,128)(2,1)S(1)}, bf16[1,2,25,12,192]{4,2,3,1,0:T(8,128)(2,1)S(1)}, u32[]{:S(2)}, u32[]{:S(2)}) %collective-permute-start.5) | collective-permute-done | bytes 230432 | tf_op jit(solution)/shard_map/ppermute | solution.py:19
  99.4 5.3 %collective-permute-done.4 = bf16[1,2,25,12,192]{4,2,3,1,0:T(8,128)(2,1)S(1)} collective-permute-done((bf16[1,2,25,12,192]{4,2,3,1,0:T(8,128)(2,1)S(1)}, bf16[1,2,25,12,192]{4,2,3,1,0:T(8,128)(2,1)S(1)}, u32[]{:S(2)}, u32[]{:S(2)}) %collective-permute-start.4) | collective-permute-done | bytes 230432 | tf_op jit(solution)/shard_map/ppermute | solution.py:21
  105.2 1.7 fusion.60
  106.9 1.9 collective-permute-start.6
  108.8 2.4 %collective-permute-start.7 = (bf16[6,1,25,12,192]{4,2,3,1,0:T(8,128)(2,1)}, bf16[6,1,25,12,192]{4,2,3,1,0:T(8,128)(2,1)}, u32[]{:S(2)}, u32[]{:S(2)}) collective-permute-start(bf16[6,1,25,12,192]{4,2,3,1,0:T(8,128)(2,1)} %get-tuple-element.18), channel_id=1, source_target_pairs={{0,1},{1,2},{2,3},{3,4},{4,5},{5,6},{6,7},{7,8},{8,9},{9,10},{10,1... | collective-permute-start | bytes 2073608 | tf_op jit(solution)/shard_map/ppermute | solution.py:19
  111.9 1.1 fusion.63
  113.0 1.8 copy.12
  114.7 17.0 %collective-permute-done.6 = bf16[6,1,25,12,192]{4,2,3,1,0:T(8,128)(2,1)} collective-permute-done((bf16[6,1,25,12,192]{4,2,3,1,0:T(8,128)(2,1)}, bf16[6,1,25,12,192]{4,2,3,1,0:T(8,128)(2,1)}, u32[]{:S(2)}, u32[]{:S(2)}) %collective-permute-start.6) | collective-permute-done | bytes 691232 | tf_op jit(solution)/shard_map/ppermute | solution.py:21
  131.8 34.7 %collective-permute-done.7 = bf16[6,1,25,12,192]{4,2,3,1,0:T(8,128)(2,1)} collective-permute-done((bf16[6,1,25,12,192]{4,2,3,1,0:T(8,128)(2,1)}, bf16[6,1,25,12,192]{4,2,3,1,0:T(8,128)(2,1)}, u32[]{:S(2)}, u32[]{:S(2)}) %collective-permute-start.7) | collective-permute-done | bytes 691232 | tf_op jit(solution)/shard_map/ppermute | solution.py:19
  166.5 3.7 %pad_maximum_fusion.4 = (bf16[4,2,25,12,192]{4,2,3,1,0:T(8,128)(2,1)}, bf16[4,2,25,12,192]{4,2,3,1,0:T(8,128)(2,1)S(1)}, bf16[4,2,25,12,192]{4,2,3,1,0:T(8,128)(2,1)}, bf16[4,2,25,12,192]{4,2,3,1,0:T(8,128)(2,1)S(1)}) fusion(bf16[6,1,25,12,192]{4,2,3,1,0:T(8,128)(2,1)} %collective-permute-done.6, bf16[1,2,25,12,192]{4,2,3,1,0:T(8,128)(2,1)} %copy-done.6, ...), kind=kLoop, calls=%fused_computation.11 | loop fusion | flops 3686400 | bytes 6451200 | tf_op jit(solution)/shard_map/concatenate | solution.py:17
  170.2 1.1 fusion.67
  171.3 1.7 copy.24
  173.1 3.5 %fusion.66 = f32[8,12,25,12]{2,1,3,0:T(8,128)} fusion(bf16[8,12,192,1]{2,1,3,0:T(8,128)(2,1)S(1)} %bitcast.166, bf16[8,25,12,192]{3,1,2,0:T(8,128)(2,1)} %bitcast.147), kind=kOutput, calls=%fused_computation.128 | convolution fusion | flops 11059200 | bytes 1073664 | tf_op jit(solution)/shard_map/nci,noei->ncoe/dot_general | solution.py:60
  176.6 2.8 %copy.21 = f32[8,12,25,12]{3,0,2,1:T(8,128)} copy(f32[8,12,25,12]{2,1,3,0:T(8,128)} %fusion.66) | data formatting | bytes 230400 | tf_op jit(solution)/shard_map/nci,noei->ncoe/dot_general | solution.py:60
  179.5 2.0 %fusion.64 = f32[8,12,25,12]{2,1,3,0:T(8,128)} fusion(bf16[8,12,192,1]{2,1,3,0:T(8,128)(2,1)S(1)} %bitcast.165, bf16[8,25,12,192]{3,1,2,0:T(8,128)(2,1)S(1)} %bitcast.146), kind=kOutput, calls=%fused_computation.126 | convolution fusion | flops 11059200 | bytes 1073664 | tf_op jit(solution)/shard_map/nci,noei->ncoe/dot_general | solution.py:60
  181.5 2.9 %copy.15 = f32[8,12,25,12]{3,0,2,1:T(8,128)} copy(f32[8,12,25,12]{2,1,3,0:T(8,128)} %fusion.64) | data formatting | bytes 230400 | tf_op jit(solution)/shard_map/nci,noei->ncoe/dot_general | solution.py:60
  184.3 2.0 %fusion.65 = f32[8,12,25,12]{2,1,3,0:T(8,128)} fusion(bf16[8,12,192,1]{2,1,3,0:T(8,128)(2,1)S(1)} %bitcast.164, bf16[8,25,12,192]{3,1,2,0:T(8,128)(2,1)S(1)} %bitcast.145), kind=kOutput, calls=%fused_computation.127 | convolution fusion | flops 11059200 | bytes 1073664 | tf_op jit(solution)/shard_map/nci,noei->ncoe/dot_general | solution.py:60
  186.4 2.9 %copy.18 = f32[8,12,25,12]{3,0,2,1:T(8,128)} copy(f32[8,12,25,12]{2,1,3,0:T(8,128)} %fusion.65) | data formatting | bytes 230400 | tf_op jit(solution)/shard_map/nci,noei->ncoe/dot_general | solution.py:60
  189.3 2.4 %pad_add_fusion = f32[8,12,7,7,12]{4,0,3,2,1:T(8,128)S(1)} fusion(f32[8,12,5,5,12]{4,0,3,2,1:T(8,128)} %bitcast.150, f32[8,12,5,5,12]{4,0,3,2,1:T(8,128)} %bitcast.151, f32[8,12,5,5,12]{4,0,3,2,1:T(8,128)} %bitcast.153, f32[8,12,5,5,12]{4,0,3,2,1:T(8,128)S(1)} %bitcast.152, f32[8,12,5,5,12]{4,0,3,2,1:T(8,128)S(1)} %bitcast.149), kind=kLoop, calls=%fused_computation.6 | loop fusion | flops 225792 | bytes 801792 | tf_op jit(solution)/shard_map/add | solution.py:103
  (49 shorter events, 6.0 us)
Async XLA Ops:
  0.0 0.9 copy-start
  0.0 29.0 %copy-start.4 = (f32[5,25,9]{2,1,0:T(8,128)S(1)}, f32[5,25,9]{2,1,0:T(8,128)}, u32[]{:S(2)}) copy-start(f32[5,25,9]{2,1,0:T(8,128)} %constant.28) | copy-start | bytes 13504
  1.4 14.5 %collective-permute-start = (bf16[1,2,5,12,192]{4,2,3,1,0:T(8,128)(2,1)S(1)}, bf16[1,2,5,12,192]{4,2,3,1,0:T(8,128)(2,1)S(1)}, u32[]{:S(2)}, u32[]{:S(2)}) collective-permute-start(bf16[1,2,5,12,192]{4,2,3,1,0:T(8,128)(2,1)S(1)} %get-tuple-element.32), channel_id=1, source_target_pairs={{0,32},{32,64},{64,96},{96,128},{128,160},{160,192},{192,224},{224... | collective-permute-start | bytes 138248 | tf_op jit(solution)/shard_map/ppermute | solution.py:19
  4.8 11.0 %collective-permute-start.1 = (bf16[1,2,5,12,192]{4,2,3,1,0:T(8,128)(2,1)S(1)}, bf16[1,2,5,12,192]{4,2,3,1,0:T(8,128)(2,1)S(1)}, u32[]{:S(2)}, u32[]{:S(2)}) collective-permute-start(bf16[1,2,5,12,192]{4,2,3,1,0:T(8,128)(2,1)S(1)} %get-tuple-element.33), channel_id=1, source_target_pairs={{32,0},{64,32},{96,64},{128,96},{160,128},{192,160},{224,192},{256... | collective-permute-start | bytes 138248 | tf_op jit(solution)/shard_map/ppermute | solution.py:21
  16.1 21.5 %collective-permute-start.3 = (bf16[6,1,5,12,192]{4,2,3,1,0:T(8,128)(2,1)S(1)}, bf16[6,1,5,12,192]{4,2,3,1,0:T(8,128)(2,1)S(1)}, u32[]{:S(2)}, u32[]{:S(2)}) collective-permute-start(bf16[6,1,5,12,192]{4,2,3,1,0:T(8,128)(2,1)S(1)} %get-tuple-element.27), channel_id=1, source_target_pairs={{1,0},{2,1},{3,2},{4,3},{5,4},{6,5},{7,6},{8,7},{9,8},{10,9},{11,1... | collective-permute-start | bytes 414728 | tf_op jit(solution)/shard_map/ppermute | solution.py:21
  27.1 14.5 %collective-permute-start.2 = (bf16[6,1,5,12,192]{4,2,3,1,0:T(8,128)(2,1)S(1)}, bf16[6,1,5,12,192]{4,2,3,1,0:T(8,128)(2,1)S(1)}, u32[]{:S(2)}, u32[]{:S(2)}) collective-permute-start(bf16[6,1,5,12,192]{4,2,3,1,0:T(8,128)(2,1)S(1)} %get-tuple-element.28), channel_id=1, source_target_pairs={{0,1},{1,2},{2,3},{3,4},{4,5},{5,6},{6,7},{7,8},{8,9},{9,10},{10,1... | collective-permute-start | bytes 414728 | tf_op jit(solution)/shard_map/ppermute | solution.py:19
  42.3 1.8 copy-start.7
  75.8 3.1 %copy-start.8 = (f32[8,5,25,1]{2,0,1,3:T(8,128)S(1)}, f32[8,5,25,1]{2,0,1,3:T(8,128)}, u32[]{:S(2)}) copy-start(f32[8,5,25,1]{2,0,1,3:T(8,128)} %convolution_bitcast_fusion) | copy-start | bytes 12004
  82.3 17.0 %collective-permute-start.5 = (bf16[1,2,25,12,192]{4,2,3,1,0:T(8,128)(2,1)S(1)}, bf16[1,2,25,12,192]{4,2,3,1,0:T(8,128)(2,1)S(1)}, u32[]{:S(2)}, u32[]{:S(2)}) collective-permute-start(bf16[1,2,25,12,192]{4,2,3,1,0:T(8,128)(2,1)S(1)} %get-tuple-element.21), channel_id=1, source_target_pairs={{0,32},{32,64},{64,96},{96,128},{128,160},{160,192},{192,224},{224... | collective-permute-start | bytes 691208 | tf_op jit(solution)/shard_map/ppermute | solution.py:19
  86.2 18.5 %collective-permute-start.4 = (bf16[1,2,25,12,192]{4,2,3,1,0:T(8,128)(2,1)S(1)}, bf16[1,2,25,12,192]{4,2,3,1,0:T(8,128)(2,1)S(1)}, u32[]{:S(2)}, u32[]{:S(2)}) collective-permute-start(bf16[1,2,25,12,192]{4,2,3,1,0:T(8,128)(2,1)S(1)} %get-tuple-element.22), channel_id=1, source_target_pairs={{32,0},{64,32},{96,64},{128,96},{160,128},{192,160},{224,192},{256... | collective-permute-start | bytes 691208 | tf_op jit(solution)/shard_map/ppermute | solution.py:21
  99.4 7.5 %copy-start.5 = (bf16[1,2,25,12,192]{4,2,3,1,0:T(8,128)(2,1)}, bf16[1,2,25,12,192]{4,2,3,1,0:T(8,128)(2,1)S(1)}, u32[]{:S(2)}) copy-start(bf16[1,2,25,12,192]{4,2,3,1,0:T(8,128)(2,1)S(1)} %collective-permute-done.5) | copy-start | bytes 691204
  104.7 2.2 %copy-start.6 = (bf16[1,2,25,12,192]{4,2,3,1,0:T(8,128)(2,1)}, bf16[1,2,25,12,192]{4,2,3,1,0:T(8,128)(2,1)S(1)}, u32[]{:S(2)}) copy-start(bf16[1,2,25,12,192]{4,2,3,1,0:T(8,128)(2,1)S(1)} %collective-permute-done.4) | copy-start | bytes 691204
  106.9 24.9 %collective-permute-start.6 = (bf16[6,1,25,12,192]{4,2,3,1,0:T(8,128)(2,1)}, bf16[6,1,25,12,192]{4,2,3,1,0:T(8,128)(2,1)}, u32[]{:S(2)}, u32[]{:S(2)}) collective-permute-start(bf16[6,1,25,12,192]{4,2,3,1,0:T(8,128)(2,1)} %get-tuple-element.17), channel_id=1, source_target_pairs={{1,0},{2,1},{3,2},{4,3},{5,4},{6,5},{7,6},{8,7},{9,8},{10,9},{11,1... | collective-permute-start | bytes 2073608 | tf_op jit(solution)/shard_map/ppermute | solution.py:21
  108.8 57.7 %collective-permute-start.7 = (bf16[6,1,25,12,192]{4,2,3,1,0:T(8,128)(2,1)}, bf16[6,1,25,12,192]{4,2,3,1,0:T(8,128)(2,1)}, u32[]{:S(2)}, u32[]{:S(2)}) collective-permute-start(bf16[6,1,25,12,192]{4,2,3,1,0:T(8,128)(2,1)} %get-tuple-element.18), channel_id=1, source_target_pairs={{0,1},{1,2},{2,3},{3,4},{4,5},{5,6},{6,7},{7,8},{8,9},{9,10},{10,1... | collective-permute-start | bytes 2073608 | tf_op jit(solution)/shard_map/ppermute | solution.py:19
  173.1 6.4 %copy-start.1 = (bf16[4,2,25,12,192]{4,2,3,1,0:T(8,128)(2,1)S(1)}, bf16[4,2,25,12,192]{4,2,3,1,0:T(8,128)(2,1)}, u32[]{:S(2)}) copy-start(bf16[4,2,25,12,192]{4,2,3,1,0:T(8,128)(2,1)} %get-tuple-element.19) | copy-start | bytes 2764804
  184.3 5.0 %copy-start.2 = (f32[8,12,25,12]{3,0,2,1:T(8,128)S(1)}, f32[8,12,25,12]{3,0,2,1:T(8,128)}, u32[]{:S(2)}) copy-start(f32[8,12,25,12]{3,0,2,1:T(8,128)} %copy.12) | copy-start | bytes 345604
  186.4 2.9 %copy-start.3 = (f32[8,12,25,12]{3,0,2,1:T(8,128)S(1)}, f32[8,12,25,12]{3,0,2,1:T(8,128)}, u32[]{:S(2)}) copy-start(f32[8,12,25,12]{3,0,2,1:T(8,128)} %copy.15) | copy-start | bytes 345604
where the time goes:
time: 195 us; the launch traced here: 194 us
  waiting for transfers between devices  73.1 us (37%)
  matrix products  38.8 us (20%)
  starting transfers between devices  38.4 us (20%)
  local copies, waits for them, and re-layouts  34.2 us (18%)
  other arithmetic  9.1 us (5%)
    ppermute x4, waiting for transfers between devices, extended(): lax.ppermute(tail, axis, [(i, (i + 1) % count) for i in range(ends)])  42.4 us
    ppermute x4, waiting for transfers between devices, extended(): lax.ppermute(head, axis, [((i + 1) % count, i) for i in range(ends)])  30.7 us
    ppermute x4, starting transfers between devices, extended(): lax.ppermute(head, axis, [((i + 1) % count, i) for i in range(ends)])  26.7 us
    gather x5, local copies, waits for them, and re-layouts, row_products(): chosen = flat_near[picked]  15.1 us
    dot_general x5, matrix products, row_products(): jnp.einsum('nqo,nqci->noci', weights, product, precision=lax.Precision.HI...  15.1 us
    dot_general x5, local copies, waits for them, and re-layouts, coarse_part(): jnp.einsum('nci,noei->ncoe', face_rows, coupled, preferred_element_type=j...  12.1 us
    ppermute x4, starting transfers between devices, extended(): lax.ppermute(tail, axis, [(i, (i + 1) % count) for i in range(ends)])  11.6 us
    dot_general x5, matrix products, coarse_part(): jnp.einsum('nci,noei->ncoe', face_rows, coupled, preferred_element_type=j...  9.8 us
  transfers between devices with their start and end apart: 8, of which 6 were waited for; matrix products, arithmetic and copies ran while one was open for 5% of the time, Pallas kernels for 0%

commit v1 on v0

v1 whole, which is shorter than its diff:
```python
import functools

import jax
import jax.numpy as jnp
from jax import lax
from jax.experimental import pallas as pl
from jax.experimental.pallas import tpu as pltpu
from jax.sharding import PartitionSpec as P

WAYS = ((-1, 0), (1, 0), (0, -1), (0, 1), (-1, -1), (-1, 1), (1, -1), (1, 1))
FACES = ((0, 0), (-1, 0), (1, 0), (0, -1), (0, 1))
SLOT = 16
WIDE = 256
COLS = 384


def spread_out(piece, face, unknowns):
    face_x, face_y = face
    lane = lax.broadcasted_iota(jnp.int32, (piece.shape[0], 128), 1)
    tiles = [None] * 5
    for step in range(5):
        source = 5 * unknowns * step
        target = 7 * unknowns * (step + 1 - face_x) + unknowns * (1 - face_y)
        width = 5 * unknowns
        for i in range(source // 128, (source + width - 1) // 128 + 1):
            turned = piece[:, 128 * i : 128 * (i + 1)]
            turn = (target - source) % 128
            if turn:
                turned = pltpu.roll(turned, turn, 1)
            first = max(source, 128 * i) - source + target
            last = min(source + width, 128 * (i + 1)) - source + target
            for j in range(first // 128, (last - 1) // 128 + 1):
                low, high = max(first - 128 * j, 0), min(last - 128 * j, 128)
                part = jnp.where((lane >= low) & (lane < high), turned, 0.0)
                tiles[j] = part if tiles[j] is None else tiles[j] + part
    zero = jnp.zeros((piece.shape[0], 128), jnp.float32)
    return [zero if tile is None else tile for tile in tiles]


def kernel(
    a_ref, a_codes, p_ref, p_codes, out_ref,
    a_buf, p_buf, near, rows_w, own, to_send, received,
    a_sem, p_sem, send_near, recv_near, send_face, recv_face,
):
    tile_x, tile_y, slots_a, edges, _ = a_ref.shape
    slots_p, unknowns = p_ref.shape[2], p_ref.shape[3]
    span = slots_p * SLOT
    at_x, at_y = lax.axis_index("gx"), lax.axis_index("gy")
    count_x, count_y = lax.axis_size("gx"), lax.axis_size("gy")

    def inside(step_x, step_y):
        there_x, there_y = at_x + step_x, at_y + step_y
        return (there_x >= 0) & (there_x < count_x) & (there_y >= 0) & (there_y < count_y)

    p_copy = pltpu.make_async_copy(p_ref, p_buf, p_sem)
    p_copy.start()
    barrier = pltpu.get_barrier_semaphore()
    neighbours = jnp.int32(0)
    for step_x, step_y in WAYS:
        there = inside(step_x, step_y)
        neighbours += there.astype(jnp.int32)

        @pl.when(there)
        def _():
            pl.semaphore_signal(
                barrier, inc=1, device_id=(at_x + step_x, at_y + step_y), device_id_type=pl.DeviceIdType.MESH
            )

    a_copies = []
    for x in range(tile_x):
        for y in range(tile_y):
            copy = pltpu.make_async_copy(a_ref.at[x, y], a_buf.at[x * tile_y + y], a_sem.at[x * tile_y + y])
            copy.start()
            a_copies.append(copy)

    for step_x, step_y in WAYS:
        @pl.when(jnp.logical_not(inside(step_x, step_y)))
        def _():
            rows = {0: slice(1, tile_y + 1), -1: slice(0, 1), 1: slice(tile_y + 1, tile_y + 2)}[step_y]
            cols = {0: slice(1, tile_x + 1), -1: slice(0, 1), 1: slice(tile_x + 1, tile_x + 2)}[step_x]
            near[rows, cols] = jnp.zeros_like(near[rows, cols])

    for way in range(4):
        step_x, step_y = WAYS[way]

        @pl.when(jnp.logical_not(inside(-step_x, -step_y)))
        def _():
            received[way] = jnp.zeros(received.shape[1:], received.dtype)

    rows_w[:, :, edges:] = jnp.zeros((rows_w.shape[0], 2 * span, WIDE - edges), jnp.bfloat16)
    near[1 : tile_y + 1, 1 : tile_x + 1] = jnp.zeros((tile_y, tile_x, span, WIDE), jnp.bfloat16)

    p_copy.wait()
    row = lax.broadcasted_iota(jnp.int32, (span, WIDE - edges), 0)
    for x in range(tile_x):
        for y in range(tile_y):
            place = row % SLOT
            for m in range(slots_p):
                code = p_codes[x, y, m]
                block = p_buf[x, y, m]
                near[y + 1, x + 1, SLOT * m : SLOT * m + unknowns, :edges] = jnp.where(
                    code < 5, block, jnp.zeros_like(block)
                )
                shift = jnp.where(code == 1, -5, jnp.where(code == 2, 5, jnp.where(code == 3, -1, jnp.where(code == 4, 1, 0))))
                place = place + jnp.where(row // SLOT == m, shift * unknowns, 0)
            near[y + 1, x + 1, :, edges:] = place.astype(jnp.float32).astype(jnp.bfloat16)

    pl.semaphore_wait(barrier, neighbours)

    def near_copy(way):
        step_x, step_y = WAYS[way]
        from_y = {0: pl.ds(1, tile_y), -1: pl.ds(1, 1), 1: pl.ds(tile_y, 1)}[step_y]
        from_x = {0: pl.ds(1, tile_x), -1: pl.ds(1, 1), 1: pl.ds(tile_x, 1)}[step_x]
        to_y = {0: pl.ds(1, tile_y), -1: pl.ds(tile_y + 1, 1), 1: pl.ds(0, 1)}[step_y]
        to_x = {0: pl.ds(1, tile_x), -1: pl.ds(tile_x + 1, 1), 1: pl.ds(0, 1)}[step_x]
        return pltpu.make_async_remote_copy(
            src_ref=near.at[from_y, from_x],
            dst_ref=near.at[to_y, to_x],
            send_sem=send_near.at[way],
            recv_sem=recv_near.at[way],
            device_id=(at_x + step_x, at_y + step_y),
            device_id_type=pl.DeviceIdType.MESH,
        )

    def face_copy(way):
        step_x, step_y = WAYS[way]
        length = tile_x if step_x == 0 else tile_y
        return pltpu.make_async_remote_copy(
            src_ref=to_send.at[way, pl.ds(0, length)],
            dst_ref=received.at[way, pl.ds(0, length)],
            send_sem=send_face.at[way],
            recv_sem=recv_face.at[way],
            device_id=(at_x + step_x, at_y + step_y),
            device_id_type=pl.DeviceIdType.MESH,
        )

    def each_way(ways, make, does, sign):
        for way in ways:
            @pl.when(inside(sign * WAYS[way][0], sign * WAYS[way][1]))
            def _():
                does(make(way))

    each_way((3, 2, 5, 7, 4, 6, 1, 0), near_copy, lambda copy: copy.start(), 1)

    def first(f, _):
        pltpu.make_async_copy(a_ref.at[0, 0], a_buf.at[f], a_sem.at[f]).wait()
        here = near[f % tile_y + 1, f // tile_y + 1, :, :edges]
        for k in range(slots_a):
            product = jnp.dot(here, a_buf[f, k], preferred_element_type=jnp.float32)
            high = product.astype(jnp.bfloat16)
            rows_w[f * slots_a + k, :span, :edges] = high
            rows_w[f * slots_a + k, span:, :edges] = (product - high.astype(jnp.float32)).astype(jnp.bfloat16)
        return 0

    lax.fori_loop(0, tile_x * tile_y, first, 0)

    each_way(range(8), near_copy, lambda copy: copy.wait_recv(), -1)

    lane = lax.broadcasted_iota(jnp.int32, (span, COLS), 1).astype(jnp.float32)

    def second(f, _):
        x, y = f // tile_y, f % tile_y
        summed = jnp.zeros((span, COLS), jnp.float32)
        for k in range(slots_a):
            code = a_codes[x, y, k]
            live = code < 9
            code = jnp.where(live, code, 4)
            step_x, step_y = code // 3 - 1, code % 3 - 1
            there = near[y + 1 + step_y, x + 1 + step_x]
            base = jnp.where(live, unknowns * (5 * (step_x + 2) + step_y + 2), -4096).astype(jnp.float32)
            both = lax.dot_general(
                rows_w[f * slots_a + k], there, (((1,), (1,)), ((), ())), preferred_element_type=jnp.float32
            )
            block = (both[:span] + both[span:]).astype(jnp.bfloat16)
            target = there[:, edges : edges + 1].astype(jnp.float32) + base
            chosen = jnp.where(lane == target, 1.0, 0.0).astype(jnp.bfloat16)
            summed += jnp.dot(block, chosen, preferred_element_type=jnp.float32)
        own[0, f] = summed[:SLOT]
        for q in range(1, 5):
            value = jnp.zeros((SLOT, COLS), jnp.float32)
            for m in range(1, slots_p):
                value += jnp.where(p_codes[x, y, m] == q, summed[SLOT * m : SLOT * (m + 1)], 0.0)
            own[q, f] = value
        return 0

    lax.fori_loop(0, tile_x * tile_y, second, 0)

    for way in range(4):
        step_x, step_y = WAYS[way]
        edge_x = range(tile_x) if step_x == 0 else (tile_x - 1 if step_x > 0 else 0,)
        edge_y = range(tile_y) if step_y == 0 else (tile_y - 1 if step_y > 0 else 0,)
        for place, (x, y) in enumerate((x, y) for x in edge_x for y in edge_y):
            to_send[way, place] = own[way + 1, x * tile_y + y].astype(jnp.bfloat16)
    each_way((3, 2, 1, 0), face_copy, lambda copy: copy.start(), 1)
    each_way(range(4), face_copy, lambda copy: copy.wait_recv(), -1)

    for x in range(tile_x):
        for y in range(tile_y):
            total = None
            for q, (face_x, face_y) in enumerate(FACES):
                from_x, from_y = x - face_x, y - face_y
                if 0 <= from_x < tile_x and 0 <= from_y < tile_y:
                    piece = own[q, from_x * tile_y + from_y]
                else:
                    piece = received[q - 1, x if face_x == 0 else y].astype(jnp.float32)
                tiles = spread_out(piece, (face_x, face_y), unknowns)
                total = tiles if total is None else [s + t for s, t in zip(total, tiles)]
            for j, tile in enumerate(total):
                high = min(128 * (j + 1), out_ref.shape[3])
                out_ref[x, y, :, 128 * j : high] = tile[:unknowns, : high - 128 * j]

    each_way(range(8), near_copy, lambda copy: copy.wait_send(), 1)
    each_way(range(4), face_copy, lambda copy: copy.wait_send(), 1)


def shards(a_blocks, a_codes, p_blocks, p_codes):
    tile_x, tile_y, slots_a = a_codes.shape
    amount = tile_x * tile_y
    slots_p, unknowns, edges = p_blocks.shape[2:]
    span = slots_p * SLOT
    longest = max(tile_x, tile_y)
    dma = pltpu.SemaphoreType.DMA
    return pl.pallas_call(
        kernel,
        out_shape=jax.ShapeDtypeStruct((tile_x, tile_y, unknowns, 49 * unknowns), jnp.float32),
        in_specs=[
            pl.BlockSpec(memory_space=pl.ANY),
            pl.BlockSpec(memory_space=pltpu.SMEM),
            pl.BlockSpec(memory_space=pl.ANY),
            pl.BlockSpec(memory_space=pltpu.SMEM),
        ],
        out_specs=pl.BlockSpec(memory_space=pltpu.VMEM),
        scratch_shapes=[
            pltpu.VMEM((amount, slots_a, edges, edges), jnp.bfloat16),
            pltpu.VMEM(p_blocks.shape, jnp.bfloat16),
            pltpu.VMEM((tile_y + 2, tile_x + 2, span, WIDE), jnp.bfloat16),
            pltpu.VMEM((amount * slots_a, 2 * span, WIDE), jnp.bfloat16),
            pltpu.VMEM((5, amount, SLOT, COLS), jnp.float32),
            pltpu.VMEM((4, longest, SLOT, COLS), jnp.bfloat16),
            pltpu.VMEM((4, longest, SLOT, COLS), jnp.bfloat16),
            dma((amount,)),
            dma,
            dma((8,)),
            dma((8,)),
            dma((4,)),
            dma((4,)),
        ],
        compiler_params=pltpu.CompilerParams(
            collective_id=0, has_side_effects=True, vmem_limit_bytes=32 * 2**20
        ),
    )(a_blocks, a_codes, p_blocks, p_codes)


def solution(mesh):
    in_specs = (
        P("gx", "gy", None, None, None),
        P("gx", "gy", None),
        P("gx", "gy", None, None, None),
        P("gx", "gy", None),
    )
    out_specs = P("gx", "gy", None, None)
    return jax.shard_map(shards, mesh=mesh, in_specs=in_specs, out_specs=out_specs, check_vma=False)
```

time: 195 us -> 43.7 us (0.22)
  waiting for transfers between devices: 73.1 us -> 0 us
  matrix products: 38.8 us -> 0 us
  starting transfers between devices: 38.4 us -> 0 us
  Pallas kernels: 0 us -> 38.1 us
  local copies, waits for them, and re-layouts: 34.2 us -> 5.32 us
  other arithmetic: 9.1 us -> 0 us
    ppermute x8 -> x0, waiting for transfers between devices: 73.1 us -> none  [the longest x4 42.4 us: extended(): lax.ppermute(tail, axis, [(i, (i + 1) % count) for i in range(ends)])]
    dot_general x21 -> x0, matrix products: 38.8 us -> none  [the longest x5 15.1 us: row_products(): jnp.einsum('nqo,nqci->noci', weights, product, precision=lax.Precision.HI...]
    ppermute x8 -> x0, starting transfers between devices: 38.4 us -> none  [the longest x4 26.7 us: extended(): lax.ppermute(head, axis, [((i + 1) % count, i) for i in range(ends)])]
    pallas_call x0 -> x1, Pallas kernels: none -> 38.1 us  [shards(): pl.pallas_call(kernel, out_shape=jax.ShapeDtypeStruct((tile_x, tile_y, un...]
    gather x5 -> x0, local copies, waits for them, and re-layouts: 15.1 us -> none  [row_products(): chosen = flat_near[picked]]
    dot_general x5 -> x0, local copies, waits for them, and re-layouts: 12.1 us -> none  [coarse_part(): jnp.einsum('nci,noei->ncoe', face_rows, coupled, preferred_element_type=j...]
    concatenate x4 -> x0, other arithmetic: 4.77 us -> none  [extended(): jnp.concatenate([lax.ppermute(tail, axis, [(i, (i + 1) % count) for i in...]
    add x1 -> x0, other arithmetic: 2.39 us -> none  [shards(): summed + coarse_part(face_rows.reshape(amount, unknowns, edges), coupled_...]
  transfers between devices with their start and end apart: 8 -> 0, of which waited for: 6 -> 0; matrix products, arithmetic and copies ran while one was open for 5% -> 0% of each run, Pallas kernels for 0% -> 0%
where the time goes in v1:
time: 43.7 us; the launch traced here: 43.5 us
  Pallas kernels  38.1 us (87%)
  local copies, waits for them, and re-layouts  5.32 us (12%)
    pallas_call x1, Pallas kernels, shards(): pl.pallas_call(kernel, out_shape=jax.ShapeDtypeStruct((tile_x, tile_y, un...  38.1 us
    unnamed x6, local copies, waits for them, and re-layouts  4.5 us

profile of v1, /device:TPU:38, one launch (start us, length us, event | category | flops | bytes accessed | tf_op | source)
XLA Modules:
  0.0 43.5 jit_solution(7048976150767252479)
XLA Ops:
  0.0 0.8 %copy.6.p_codes = s32[4,2,3]{2,1,0:T(2,128)S(1)} copy(s32[4,2,3]{0,1,2:T(2,128)} %param.7) | data formatting | bytes 192 | tf_op args[3]
  0.8 0.9 %copy.5.p_ref = bf16[4,2,3,12,192]{4,3,2,1,0:T(8,128)(2,1)S(1)} copy(bf16[4,2,3,12,192]{4,1,3,2,0:T(2,128)(2,1)} %param.6) | data formatting | bytes 221184 | tf_op args[2]
  1.7 0.0 copy-start
  1.7 2.1 %copy-done = bf16[4,2,5,192,192]{4,3,2,1,0:T(8,128)(2,1)S(1)} copy-done((bf16[4,2,5,192,192]{4,3,2,1,0:T(8,128)(2,1)S(1)}, bf16[4,2,5,192,192]{4,3,2,1,0:T(8,128)(2,1)}, u32[]{:S(2)}) %copy-start) | copy-done | bytes 2949144
  3.8 0.0 copy-start.1
  3.8 0.7 %copy-done.1 = s32[4,2,5]{2,1,0:T(2,128)S(1)} copy-done((s32[4,2,5]{2,1,0:T(2,128)S(1)}, s32[4,2,5]{2,1,0:T(2,128)}, u32[]{:S(2)}) %copy-start.1) | copy-done | bytes 184
  4.5 38.1 %shard_map.46 = f32[4,2,12,588]{3,2,1,0:T(8,128)S(1)} custom-call(bf16[4,2,5,192,192]{4,3,2,1,0:T(8,128)(2,1)S(1)} %copy-done, s32[4,2,5]{2,1,0:T(2,128)S(1)} %copy-done.1, bf16[4,2,3,12,192]{4,3,2,1,0:T(8,128)(2,1)S(1)} %copy.5.p_ref, s32[4,2,3]{2,1,0:T(2,128)S(1)} %copy.6.p_codes), custom_call_target="tpu_custom_call" | custom-call | tf_op jit(solution)/shard_map/pallas_call | solution.py:223
  42.7 0.8 %copy.7 = f32[4,2,12,588]{3,1,2,0:T(2,128)} copy(f32[4,2,12,588]{3,2,1,0:T(8,128)S(1)} %shard_map.46) | data formatting | bytes 451584 | tf_op jit(solution)/shard_map/pallas_call | solution.py:223
Async XLA Ops:
  1.7 2.1 %copy-start = (bf16[4,2,5,192,192]{4,3,2,1,0:T(8,128)(2,1)S(1)}, bf16[4,2,5,192,192]{4,3,2,1,0:T(8,128)(2,1)}, u32[]{:S(2)}) copy-start(bf16[4,2,5,192,192]{4,3,2,1,0:T(8,128)(2,1)} %a_ref.1) | copy-start | bytes 8847364
  3.8 0.7 %copy-start.1 = (s32[4,2,5]{2,1,0:T(2,128)S(1)}, s32[4,2,5]{2,1,0:T(2,128)}, u32[]{:S(2)}) copy-start(s32[4,2,5]{2,1,0:T(2,128)} %a_codes.1) | copy-start | bytes 484

commit v2 on v1

v2 whole, which is shorter than its diff:
```python
import functools

import jax
import jax.numpy as jnp
from jax import lax
from jax.experimental import pallas as pl
from jax.experimental.pallas import tpu as pltpu
from jax.sharding import PartitionSpec as P

WAYS = ((-1, 0), (1, 0), (0, -1), (0, 1), (-1, -1), (-1, 1), (1, -1), (1, 1))
FACES = ((0, 0), (-1, 0), (1, 0), (0, -1), (0, 1))
SLOT = 16
WIDE = 256
COLS = 384


def spread_out(piece, face, unknowns):
    face_x, face_y = face
    lane = lax.broadcasted_iota(jnp.int32, (piece.shape[0], 128), 1)
    tiles = [None] * 5
    for step in range(5):
        source = 5 * unknowns * step
        target = 7 * unknowns * (step + 1 - face_x) + unknowns * (1 - face_y)
        width = 5 * unknowns
        for i in range(source // 128, (source + width - 1) // 128 + 1):
            turned = piece[:, 128 * i : 128 * (i + 1)]
            turn = (target - source) % 128
            if turn:
                turned = pltpu.roll(turned, turn, 1)
            first = max(source, 128 * i) - source + target
            last = min(source + width, 128 * (i + 1)) - source + target
            for j in range(first // 128, (last - 1) // 128 + 1):
                low, high = max(first - 128 * j, 0), min(last - 128 * j, 128)
                part = jnp.where((lane >= low) & (lane < high), turned, 0.0)
                tiles[j] = part if tiles[j] is None else tiles[j] + part
    zero = jnp.zeros((piece.shape[0], 128), jnp.float32)
    return [zero if tile is None else tile for tile in tiles]


def kernel(
    a_ref, a_codes, p_ref, p_codes, out_ref,
    a_buf, p_buf, mid, inner_side, outer_side, rows_w, own, send_y, got_y, send_x, got_x,
    a_sem, p_sem, side_out, side_in, mid_out, mid_in, y_out, y_in, x_out, x_in,
):
    tile_x, tile_y, slots_a, edges, _ = a_ref.shape
    slots_p, unknowns = p_ref.shape[1], p_ref.shape[2]
    span = slots_p * SLOT
    at_x, at_y = lax.axis_index("gx"), lax.axis_index("gy")
    count_x, count_y = lax.axis_size("gx"), lax.axis_size("gy")
    outer = at_y % 2
    inner = 1 - outer
    rows = (inner, outer)
    sides = (inner_side, outer_side)

    def inside(step_x, step_y):
        there_x, there_y = at_x + step_x, at_y + step_y
        return (there_x >= 0) & (there_x < count_x) & (there_y >= 0) & (there_y < count_y)

    p_copy = pltpu.make_async_copy(p_ref, p_buf, p_sem)
    p_copy.start()
    barrier = pltpu.get_barrier_semaphore()
    neighbours = jnp.int32(0)
    for step_x, step_y in WAYS:
        there = inside(step_x, step_y)
        neighbours += there.astype(jnp.int32)

        @pl.when(there)
        def _():
            pl.semaphore_signal(
                barrier, inc=1, device_id=(at_x + step_x, at_y + step_y), device_id_type=pl.DeviceIdType.MESH
            )

    def a_copy(x, y):
        return pltpu.make_async_copy(a_ref.at[x, y], a_buf.at[x, y], a_sem.at[x, y])

    for y in (inner, outer):
        for x in range(tile_x):
            a_copy(x, y).start()

    for way in range(2):
        @pl.when(jnp.logical_not(inside(1 - 2 * way, 0)))
        def _():
            column = (tile_x + 1) * (1 - way)
            mid[:, column] = jnp.zeros((tile_y, span, WIDE), jnp.bfloat16)
            got_x[way] = jnp.zeros(got_x.shape[1:], got_x.dtype)

    for side in range(2):
        step_y = 2 * rows[side] - 1
        for step_x in (-1, 0, 1):
            @pl.when(jnp.logical_not(inside(step_x, step_y)))
            def _():
                columns = {0: slice(1, tile_x + 1), -1: slice(0, 1), 1: slice(tile_x + 1, tile_x + 2)}[step_x]
                sides[side][columns] = jnp.zeros_like(sides[side][columns])
                if step_x == 0:
                    got_y[side] = jnp.zeros(got_y.shape[1:], got_y.dtype)

    rows_w[:, :, :, :, edges:] = jnp.zeros((tile_x, tile_y, slots_a, 2 * span, WIDE - edges), jnp.bfloat16)

    p_copy.wait()
    taken = slots_p * unknowns * tile_y
    target_row = lax.broadcasted_iota(jnp.int32, (tile_y * span, taken), 0)
    source_row = lax.broadcasted_iota(jnp.int32, (tile_y * span, taken), 1)
    row = lax.broadcasted_iota(jnp.int32, (span, WIDE - edges), 0)
    for x in range(tile_x):
        wanted = jnp.full_like(target_row, -1)
        for y in range(tile_y):
            place = row % SLOT
            for m in range(slots_p):
                code = p_codes[m, y, x]
                first_row = y * span + m * SLOT
                fits = (target_row >= first_row) & (target_row < first_row + unknowns) & (code < 5)
                wanted = jnp.where(fits, (target_row - first_row + m * unknowns) * tile_y + y, wanted)
                shift = jnp.where(code == 1, -5, jnp.where(code == 2, 5, jnp.where(code == 3, -1, jnp.where(code == 4, 1, 0))))
                place = place + jnp.where(row // SLOT == m, shift * unknowns, 0)
            mid[y, x + 1, :, edges:] = place.astype(jnp.float32).astype(jnp.bfloat16)
        order = jnp.where(wanted == source_row, 1.0, 0.0).astype(jnp.bfloat16)
        laid = jnp.dot(order, p_buf[x].reshape(taken, edges), preferred_element_type=jnp.float32).astype(jnp.bfloat16)
        for y in range(tile_y):
            mid[y, x + 1, :, :edges] = laid[y * span : (y + 1) * span]

    def side_copy(step_x, side):
        source = {0: pl.ds(1, tile_x), -1: pl.ds(1, 1), 1: pl.ds(tile_x, 1)}[step_x]
        target = {0: pl.ds(1, tile_x), -1: pl.ds(tile_x + 1, 1), 1: pl.ds(0, 1)}[step_x]
        return pltpu.make_async_remote_copy(
            src_ref=mid.at[rows[side], source],
            dst_ref=sides[side].at[target],
            send_sem=side_out.at[side, step_x + 1],
            recv_sem=side_in.at[side, step_x + 1],
            device_id=(at_x + step_x, at_y + 2 * rows[side] - 1),
            device_id_type=pl.DeviceIdType.MESH,
        )

    def mid_copy(way):
        return pltpu.make_async_remote_copy(
            src_ref=mid.at[:, pl.ds(1 + (tile_x - 1) * way, 1)],
            dst_ref=mid.at[:, pl.ds((tile_x + 1) * (1 - way), 1)],
            send_sem=mid_out.at[way],
            recv_sem=mid_in.at[way],
            device_id=(at_x + 2 * way - 1, at_y),
            device_id_type=pl.DeviceIdType.MESH,
        )

    def y_copy(side):
        return pltpu.make_async_remote_copy(
            src_ref=send_y.at[side],
            dst_ref=got_y.at[side],
            send_sem=y_out.at[side],
            recv_sem=y_in.at[side],
            device_id=(at_x, at_y + 2 * rows[side] - 1),
            device_id_type=pl.DeviceIdType.MESH,
        )

    def x_copy(way, side):
        return pltpu.make_async_remote_copy(
            src_ref=send_x.at[way, side],
            dst_ref=got_x.at[way, side],
            send_sem=x_out.at[way, side],
            recv_sem=x_in.at[way, side],
            device_id=(at_x + 2 * way - 1, at_y),
            device_id_type=pl.DeviceIdType.MESH,
        )

    def when_inside(step_x, step_y, does):
        pl.when(inside(step_x, step_y))(does)

    def first(y):
        for x in range(tile_x):
            a_copy(x, y).wait()
            here = mid[y, x + 1, :, :edges]
            for k in range(slots_a):
                product = jnp.dot(here, a_buf[x, y, k], preferred_element_type=jnp.float32)
                high = product.astype(jnp.bfloat16)
                rows_w[x, y, k, :span, :edges] = high
                rows_w[x, y, k, span:, :edges] = (product - high.astype(jnp.float32)).astype(jnp.bfloat16)

    lane = lax.broadcasted_iota(jnp.int32, (span, COLS), 1).astype(jnp.float32)

    def second(side):
        y = rows[side]
        for x in range(tile_x):
            summed = jnp.zeros((span, COLS), jnp.float32)
            for k in range(slots_a):
                code = a_codes[x, y, k]
                live = code < 9
                code = jnp.where(live, code, 4)
                step_x, step_y = code // 3 - 1, code % 3 - 1
                there = jnp.where(
                    step_y == 2 * y - 1,
                    sides[side][x + 1 + step_x],
                    mid[jnp.clip(y + step_y, 0, tile_y - 1), x + 1 + step_x],
                )
                base = jnp.where(live, unknowns * (5 * (step_x + 2) + step_y + 2), -4096).astype(jnp.float32)
                both = lax.dot_general(
                    rows_w[x, y, k], there, (((1,), (1,)), ((), ())), preferred_element_type=jnp.float32
                )
                block = (both[:span] + both[span:]).astype(jnp.bfloat16)
                target = there[:, edges : edges + 1].astype(jnp.float32) + base
                chosen = jnp.where(lane == target, 1.0, 0.0).astype(jnp.bfloat16)
                summed += jnp.dot(block, chosen, preferred_element_type=jnp.float32)
            own[0, x, y] = summed[:SLOT]
            for q in range(1, 5):
                value = jnp.zeros((SLOT, COLS), jnp.float32)
                for m in range(1, slots_p):
                    value += jnp.where(p_codes[m, y, x] == q, summed[SLOT * m : SLOT * (m + 1)], 0.0)
                own[q, x, y] = value

    def send_contributions(side):
        y = rows[side]
        for x in range(tile_x):
            send_y[side, x] = own[y + 3, x, y].astype(jnp.bfloat16)
        when_inside(0, 2 * y - 1, lambda: y_copy(side).start())
        for way in range(2):
            send_x[way, side] = own[way + 1, (tile_x - 1) * way, y].astype(jnp.bfloat16)
            when_inside(2 * way - 1, 0, lambda: x_copy(way, side).start())

    pl.semaphore_wait(barrier, neighbours)
    for step_x in (0, -1, 1):
        when_inside(step_x, 2 * outer - 1, lambda: side_copy(step_x, 1).start())
    for way in range(2):
        when_inside(2 * way - 1, 0, lambda: mid_copy(way).start())
    for step_x in (0, -1, 1):
        when_inside(step_x, 2 * inner - 1, lambda: side_copy(step_x, 0).start())

    def both_firsts(i, _):
        first(jnp.where(i == 0, inner, outer))
        return 0

    lax.fori_loop(0, 2, both_firsts, 0)

    for way in range(2):
        when_inside(1 - 2 * way, 0, lambda: mid_copy(way).wait_recv())
    for side in range(2):
        for step_x in (0, -1, 1):
            when_inside(-step_x, 2 * rows[side] - 1, lambda: side_copy(step_x, side).wait_recv())
        second(side)
        send_contributions(side)

    def put(x, y, pieces, add):
        total = None
        for piece, face in pieces:
            tiles = spread_out(piece.astype(jnp.float32), FACES[face], unknowns)
            total = tiles if total is None else [s + t for s, t in zip(total, tiles)]
        for j, tile in enumerate(total):
            high = min(128 * (j + 1), out_ref.shape[3])
            tile = tile[:unknowns, : high - 128 * j]
            if add:
                tile = tile + out_ref[x, y, :, 128 * j : high]
            out_ref[x, y, :, 128 * j : high] = tile

    for x in range(tile_x):
        for y in range(tile_y):
            pieces = []
            for face, (face_x, face_y) in enumerate(FACES):
                from_x, from_y = x - face_x, y - face_y
                if 0 <= from_x < tile_x and 0 <= from_y < tile_y:
                    pieces.append((own[face, from_x, from_y], face))
            put(x, y, pieces, False)

    for way in range(2):
        for side in range(2):
            when_inside(1 - 2 * way, 0, lambda: x_copy(way, side).wait_recv())
    for side in range(2):
        when_inside(0, 2 * rows[side] - 1, lambda: y_copy(side).wait_recv())

    for x in range(tile_x):
        for y in range(tile_y):
            side = outer if y else inner
            pieces = [(got_y[side, x], 4 - y)]
            if x == 0:
                pieces.append((got_x[1, side], 2))
            if x == tile_x - 1:
                pieces.append((got_x[0, side], 1))
            put(x, y, pieces, True)

    for side in range(2):
        for step_x in (-1, 0, 1):
            when_inside(step_x, 2 * rows[side] - 1, lambda: side_copy(step_x, side).wait_send())
        when_inside(0, 2 * rows[side] - 1, lambda: y_copy(side).wait_send())
        for way in range(2):
            when_inside(2 * way - 1, 0, lambda: x_copy(way, side).wait_send())
    for way in range(2):
        when_inside(2 * way - 1, 0, lambda: mid_copy(way).wait_send())


def shards(a_blocks, a_codes, p_blocks, p_codes):
    tile_x, tile_y, slots_a = a_codes.shape
    slots_p, unknowns, edges = p_blocks.shape[2:]
    span = slots_p * SLOT
    dma = pltpu.SemaphoreType.DMA
    return pl.pallas_call(
        kernel,
        out_shape=jax.ShapeDtypeStruct((tile_x, tile_y, unknowns, 49 * unknowns), jnp.float32),
        in_specs=[
            pl.BlockSpec(memory_space=pltpu.HBM),
            pl.BlockSpec(memory_space=pltpu.SMEM),
            pl.BlockSpec(memory_space=pltpu.HBM),
            pl.BlockSpec(memory_space=pltpu.SMEM),
        ],
        out_specs=pl.BlockSpec(memory_space=pltpu.VMEM),
        scratch_shapes=[
            pltpu.VMEM((tile_x, tile_y, slots_a, edges, edges), jnp.bfloat16),
            pltpu.VMEM((tile_x, slots_p, unknowns, tile_y, edges), jnp.bfloat16),
            pltpu.VMEM((tile_y, tile_x + 2, span, WIDE), jnp.bfloat16),
            pltpu.VMEM((tile_x + 2, span, WIDE), jnp.bfloat16),
            pltpu.VMEM((tile_x + 2, span, WIDE), jnp.bfloat16),
            pltpu.VMEM((tile_x, tile_y, slots_a, 2 * span, WIDE), jnp.bfloat16),
            pltpu.VMEM((5, tile_x, tile_y, SLOT, COLS), jnp.float32),
            pltpu.VMEM((tile_y, tile_x, SLOT, COLS), jnp.bfloat16),
            pltpu.VMEM((tile_y, tile_x, SLOT, COLS), jnp.bfloat16),
            pltpu.VMEM((2, tile_y, SLOT, COLS), jnp.bfloat16),
            pltpu.VMEM((2, tile_y, SLOT, COLS), jnp.bfloat16),
            dma((tile_x, tile_y)),
            dma,
            dma((2, 3)),
            dma((2, 3)),
            dma((2,)),
            dma((2,)),
            dma((2,)),
            dma((2,)),
            dma((2, 2)),
            dma((2, 2)),
        ],
        compiler_params=pltpu.CompilerParams(
            collective_id=0, has_side_effects=True, vmem_limit_bytes=40 * 2**20
        ),
    )(pltpu.with_memory_space_constraint(a_blocks, pltpu.HBM), pltpu.with_memory_space_constraint(a_codes, pltpu.HBM), pltpu.with_memory_space_constraint(jnp.transpose(p_blocks, (0, 2, 3, 1, 4)), pltpu.HBM), pltpu.with_memory_space_constraint(jnp.transpose(p_codes, (2, 1, 0)), pltpu.HBM))


def solution(mesh):
    in_specs = (
        P("gx", "gy", None, None, None),
        P("gx", "gy", None),
        P("gx", "gy", None, None, None),
        P("gx", "gy", None),
    )
    out_specs = P("gx", "gy", None, None)
    return jax.shard_map(shards, mesh=mesh, in_specs=in_specs, out_specs=out_specs, check_vma=False)
```

time: 43.7 us -> 35.3 us (0.81)
  the two profiles are of different devices: /device:TPU:38 before, /device:TPU:33 now
where the time goes in v2:
time: 35.3 us; the launch traced here: 35.2 us
  Pallas kernels  34.4 us (97%)
  local copies, waits for them, and re-layouts  0.82 us (2%)
    pallas_call x1, Pallas kernels, shards(): pl.pallas_call(kernel, out_shape=jax.ShapeDtypeStruct((tile_x, tile_y, un...  34.4 us
    pallas_call x1, local copies, waits for them, and re-layouts, shards(): pl.pallas_call(kernel, out_shape=jax.ShapeDtypeStruct((tile_x, tile_y, un...  0.82 us

profile of v2, /device:TPU:33, one launch (start us, length us, event | category | flops | bytes accessed | tf_op | source)
XLA Modules:
  0.0 35.2 jit_solution(5376946836220690953)
XLA Ops:
  0.0 34.4 %shard_map.46 = f32[4,2,12,588]{3,2,1,0:T(8,128)S(1)} custom-call(bf16[4,2,5,192,192]{4,3,2,1,0:T(8,128)(2,1)} %a_ref.1, s32[4,2,5]{2,1,0:T(2,128)} %a_codes.1, bf16[4,3,12,2,192]{4,3,2,1,0:T(2,128)(2,1)} %bitcast.2, s32[3,2,4]{2,1,0:T(2,128)} %bitcast.3), custom_call_target="tpu_custom_call" | custom-call | tf_op jit(solution)/shard_map/pallas_call | solution.py:290
  34.4 0.8 %copy.5 = f32[4,2,12,588]{3,1,2,0:T(2,128)} copy(f32[4,2,12,588]{3,2,1,0:T(8,128)S(1)} %shard_map.46) | data formatting | bytes 451584 | tf_op jit(solution)/shard_map/pallas_call | solution.py:290

commit v3 on v2

--- a/solution.py
+++ b/solution.py
@@ -11,6 +11,7 @@
 FACES = ((0, 0), (-1, 0), (1, 0), (0, -1), (0, 1))
 SLOT = 16
 WIDE = 256
+PACK = 64
 COLS = 384
 
 
@@ -37,9 +38,53 @@
     return [zero if tile is None else tile for tile in tiles]
 
 
+def one_hot(wanted, source):
+    return jnp.where(wanted == source, 1.0, 0.0).astype(jnp.bfloat16)
+
+
+def pack(block, slots, unknowns):
+    span, used = block.shape[0], slots * unknowns
+    lane = lax.broadcasted_iota(jnp.int32, (span, 128), 1)
+    rest = block[:, 128:].astype(jnp.float32)
+    turned = pltpu.roll(rest, 64, 1)
+    zero = jnp.zeros_like(rest)
+    parts = [jnp.where(lane < 64, rest, zero), jnp.where(lane < 64, zero, turned), jnp.where(lane < 64, turned, rest)]
+    stacked = jnp.concatenate([block[:, :128]] + [part.astype(jnp.bfloat16) for part in parts], axis=0)
+    row = lax.broadcasted_iota(jnp.int32, (PACK, 4 * span), 0)
+    source = lax.broadcasted_iota(jnp.int32, (PACK, 4 * span), 1)
+    part, at = source // span, source % span
+    dense = at // SLOT * unknowns + at % SLOT
+    dense = jnp.where(at % SLOT < unknowns, dense, -1)
+    half = used // 2
+    low = jnp.where((dense >= 0) & (dense < half), used + dense, -1)
+    high = jnp.where(dense >= half, used + dense - half, -1)
+    mark = jnp.where(at % SLOT == 0, used + half + at // SLOT, -1)
+    goes = jnp.where(part == 0, dense, jnp.where(part == 1, low, jnp.where(part == 2, high, mark)))
+    return jnp.dot(one_hot(goes, row), stacked, preferred_element_type=jnp.float32).astype(jnp.bfloat16)
+
+
+def unpack(packed, slots, unknowns):
+    span, used = slots * SLOT, slots * unknowns
+    row = lax.broadcasted_iota(jnp.int32, (3 * span, PACK), 0)
+    source = lax.broadcasted_iota(jnp.int32, (3 * span, PACK), 1)
+    part, at = row // span, row % span
+    dense = at // SLOT * unknowns + at % SLOT
+    half = used // 2
+    folded = used + jnp.where(dense < half, dense, dense - half)
+    comes = jnp.where(part == 0, dense, jnp.where(part == 1, folded, used + half + at // SLOT))
+    comes = jnp.where((at % SLOT < unknowns) | (part == 2), comes, -1)
+    laid = jnp.dot(one_hot(comes, source), packed, preferred_element_type=jnp.float32)
+    lane = lax.broadcasted_iota(jnp.int32, (span, 128), 1)
+    at = lax.broadcasted_iota(jnp.int32, (span, 128), 0)
+    rest = laid[span : 2 * span]
+    rest = jnp.where(at // SLOT * unknowns + at % SLOT < half, rest, pltpu.roll(rest, 64, 1))
+    rest = jnp.where(lane < 64, rest, laid[2 * span :] + (at % SLOT).astype(jnp.float32))
+    return laid[:span].astype(jnp.bfloat16), rest.astype(jnp.bfloat16)
+
+
 def kernel(
     a_ref, a_codes, p_ref, p_codes, out_ref,
-    a_buf, p_buf, mid, inner_side, outer_side, rows_w, own, send_y, got_y, send_x, got_x,
+    a_buf, p_buf, mid, inner_side, outer_side, packed, got, rows_w, own, send_y, got_y, send_x, got_x,
     a_sem, p_sem, side_out, side_in, mid_out, mid_in, y_out, y_in, x_out, x_in,
 ):
     tile_x, tile_y, slots_a, edges, _ = a_ref.shape
@@ -90,7 +135,8 @@
             @pl.when(jnp.logical_not(inside(step_x, step_y)))
             def _():
                 columns = {0: slice(1, tile_x + 1), -1: slice(0, 1), 1: slice(tile_x + 1, tile_x + 2)}[step_x]
-                sides[side][columns] = jnp.zeros_like(sides[side][columns])
+                holds = got if side else inner_side
+                holds[columns] = jnp.zeros_like(holds[columns])
                 if step_x == 0:
                     got_y[side] = jnp.zeros(got_y.shape[1:], got_y.dtype)
 
@@ -122,8 +168,8 @@
         source = {0: pl.ds(1, tile_x), -1: pl.ds(1, 1), 1: pl.ds(tile_x, 1)}[step_x]
         target = {0: pl.ds(1, tile_x), -1: pl.ds(tile_x + 1, 1), 1: pl.ds(0, 1)}[step_x]
         return pltpu.make_async_remote_copy(
-            src_ref=mid.at[rows[side], source],
-            dst_ref=sides[side].at[target],
+            src_ref=packed.at[pl.ds(source.start - 1, source.size)] if side else mid.at[inner, source],
+            dst_ref=(got if side else inner_side).at[target],
             send_sem=side_out.at[side, step_x + 1],
             recv_sem=side_in.at[side, step_x + 1],
             device_id=(at_x + step_x, at_y + 2 * rows[side] - 1),
@@ -213,6 +259,9 @@
             send_x[way, side] = own[way + 1, (tile_x - 1) * way, y].astype(jnp.bfloat16)
             when_inside(2 * way - 1, 0, lambda: x_copy(way, side).start())
 
+    for x in range(tile_x):
+        packed[x] = pack(mid[outer, x + 1], slots_p, unknowns)
+
     pl.semaphore_wait(barrier, neighbours)
     for step_x in (0, -1, 1):
         when_inside(step_x, 2 * outer - 1, lambda: side_copy(step_x, 1).start())
@@ -232,6 +281,9 @@
     for side in range(2):
         for step_x in (0, -1, 1):
             when_inside(-step_x, 2 * rows[side] - 1, lambda: side_copy(step_x, side).wait_recv())
+        if side:
+            for x in range(tile_x + 2):
+                outer_side[x, :, :128], outer_side[x, :, 128:] = unpack(got[x], slots_p, unknowns)
         second(side)
         send_contributions(side)
 
@@ -303,6 +355,8 @@
             pltpu.VMEM((tile_y, tile_x + 2, span, WIDE), jnp.bfloat16),
             pltpu.VMEM((tile_x + 2, span, WIDE), jnp.bfloat16),
             pltpu.VMEM((tile_x + 2, span, WIDE), jnp.bfloat16),
+            pltpu.VMEM((tile_x, PACK, 128), jnp.bfloat16),
+            pltpu.VMEM((tile_x + 2, PACK, 128), jnp.bfloat16),
             pltpu.VMEM((tile_x, tile_y, slots_a, 2 * span, WIDE), jnp.bfloat16),
             pltpu.VMEM((5, tile_x, tile_y, SLOT, COLS), jnp.float32),
             pltpu.VMEM((tile_y, tile_x, SLOT, COLS), jnp.bfloat16),

time: 35.3 us -> 32.4 us (0.918)
  the two profiles are of different devices: /device:TPU:33 before, /device:TPU:35 now
where the time goes in v3:
time: 32.4 us; the launch traced here: 32.3 us
  Pallas kernels  31.5 us (97%)
  local copies, waits for them, and re-layouts  0.82 us (3%)
    pallas_call x1, Pallas kernels, shards(): pl.pallas_call(kernel, out_shape=jax.ShapeDtypeStruct((tile_x, tile_y, un...  31.5 us
    pallas_call x1, local copies, waits for them, and re-layouts, shards(): pl.pallas_call(kernel, out_shape=jax.ShapeDtypeStruct((tile_x, tile_y, un...  0.82 us

profile of v3, /device:TPU:35, one launch (start us, length us, event | category | flops | bytes accessed | tf_op | source)
XLA Modules:
  0.0 32.3 jit_solution(17919687970299542867)
XLA Ops:
  0.0 31.5 %shard_map.46 = f32[4,2,12,588]{3,2,1,0:T(8,128)S(1)} custom-call(bf16[4,2,5,192,192]{4,3,2,1,0:T(8,128)(2,1)} %a_ref.1, s32[4,2,5]{2,1,0:T(2,128)} %a_codes.1, bf16[4,3,12,2,192]{4,3,2,1,0:T(2,128)(2,1)} %bitcast.2, s32[3,2,4]{2,1,0:T(2,128)} %bitcast.3), custom_call_target="tpu_custom_call" | custom-call | tf_op jit(solution)/shard_map/pallas_call | solution.py:342
  31.5 0.8 %copy.5 = f32[4,2,12,588]{3,1,2,0:T(2,128)} copy(f32[4,2,12,588]{3,2,1,0:T(8,128)S(1)} %shard_map.46) | data formatting | bytes 451584 | tf_op jit(solution)/shard_map/pallas_call | solution.py:342

commit v4 on v3

--- a/solution.py
+++ b/solution.py
@@ -85,7 +85,7 @@
 def kernel(
     a_ref, a_codes, p_ref, p_codes, out_ref,
     a_buf, p_buf, mid, inner_side, outer_side, packed, got, rows_w, own, send_y, got_y, send_x, got_x,
-    a_sem, p_sem, side_out, side_in, mid_out, mid_in, y_out, y_in, x_out, x_in,
+    a_sem, p_sem, side_out, side_in, mid_out, mid_in, y_out, y_in, x_out, x_in, ready,
 ):
     tile_x, tile_y, slots_a, edges, _ = a_ref.shape
     slots_p, unknowns = p_ref.shape[1], p_ref.shape[2]
@@ -103,13 +103,21 @@
 
     p_copy = pltpu.make_async_copy(p_ref, p_buf, p_sem)
     p_copy.start()
+    def start_order(x, y):
+        z = y // 2 % 4 * 4 + x // 4
+        return (jnp.where(z < 8, 2 * z, jnp.where(z < 12, 16, 15)) + x % 4 + y // 8) * 1024 + x * 32 + y
+
+    def later(step_x, step_y):
+        return start_order(at_x + step_x, at_y + step_y) > start_order(at_x, at_y)
+
     barrier = pltpu.get_barrier_semaphore()
-    neighbours = jnp.int32(0)
+    earlier_ones = jnp.int32(0)
     for step_x, step_y in WAYS:
         there = inside(step_x, step_y)
-        neighbours += there.astype(jnp.int32)
-
-        @pl.when(there)
+        comes_later = later(step_x, step_y)
+        earlier_ones += (there & jnp.logical_not(comes_later)).astype(jnp.int32)
+
+        @pl.when(there & comes_later)
         def _():
             pl.semaphore_signal(
                 barrier, inc=1, device_id=(at_x + step_x, at_y + step_y), device_id_type=pl.DeviceIdType.MESH
@@ -141,6 +149,17 @@
                     got_y[side] = jnp.zeros(got_y.shape[1:], got_y.dtype)
 
     rows_w[:, :, :, :, edges:] = jnp.zeros((tile_x, tile_y, slots_a, 2 * span, WIDE - edges), jnp.bfloat16)
+
+    pl.when(earlier_ones > 0)(lambda: pl.semaphore_wait(barrier, earlier_ones))
+    for step_x, step_y in WAYS:
+        @pl.when(inside(step_x, step_y) & jnp.logical_not(later(step_x, step_y)))
+        def _():
+            pl.semaphore_signal(
+                ready.at[(1 - step_x) * 3 + 1 - step_y],
+                inc=1,
+                device_id=(at_x + step_x, at_y + step_y),
+                device_id_type=pl.DeviceIdType.MESH,
+            )
 
     p_copy.wait()
     taken = slots_p * unknowns * tile_y
@@ -262,13 +281,16 @@
     for x in range(tile_x):
         packed[x] = pack(mid[outer, x + 1], slots_p, unknowns)
 
-    pl.semaphore_wait(barrier, neighbours)
-    for step_x in (0, -1, 1):
-        when_inside(step_x, 2 * outer - 1, lambda: side_copy(step_x, 1).start())
-    for way in range(2):
-        when_inside(2 * way - 1, 0, lambda: mid_copy(way).start())
-    for step_x in (0, -1, 1):
-        when_inside(step_x, 2 * inner - 1, lambda: side_copy(step_x, 0).start())
+    outer_copies = [(step_x, 2 * outer - 1, functools.partial(side_copy, step_x, 1)) for step_x in (0, -1, 1)]
+    inner_copies = [(step_x, 2 * inner - 1, functools.partial(side_copy, step_x, 0)) for step_x in (0, -1, 1)]
+    mid_copies = [(2 * way - 1, 0, functools.partial(mid_copy, way)) for way in range(2)]
+    for step_x, step_y, copy in outer_copies + mid_copies + inner_copies:
+        pl.when(inside(step_x, step_y) & jnp.logical_not(later(step_x, step_y)))(lambda: copy().start())
+    for step_x, step_y, copy in mid_copies + inner_copies + outer_copies:
+        @pl.when(inside(step_x, step_y) & later(step_x, step_y))
+        def _():
+            pl.semaphore_wait(ready.at[(step_x + 1) * 3 + step_y + 1], 1)
+            copy().start()
 
     def both_firsts(i, _):
         first(jnp.where(i == 0, inner, outer))
@@ -373,6 +395,7 @@
             dma((2,)),
             dma((2, 2)),
             dma((2, 2)),
+            pltpu.SemaphoreType.REGULAR((9,)),
         ],
         compiler_params=pltpu.CompilerParams(
             collective_id=0, has_side_effects=True, vmem_limit_bytes=40 * 2**20

time: 32.4 us -> 31.6 us (0.975)
  the two profiles are of different devices: /device:TPU:35 before, /device:TPU:34 now
where the time goes in v4:
time: 31.6 us; the launch traced here: 31.4 us
  Pallas kernels  30.6 us (97%)
  local copies, waits for them, and re-layouts  0.82 us (3%)
    pallas_call x1, Pallas kernels, shards(): pl.pallas_call(kernel, out_shape=jax.ShapeDtypeStruct((tile_x, tile_y, un...  30.6 us
    pallas_call x1, local copies, waits for them, and re-layouts, shards(): pl.pallas_call(kernel, out_shape=jax.ShapeDtypeStruct((tile_x, tile_y, un...  0.82 us

profile of v4, /device:TPU:34, one launch (start us, length us, event | category | flops | bytes accessed | tf_op | source)
XLA Modules:
  0.0 31.4 jit_solution(14118397734179208887)
XLA Ops:
  0.0 30.6 %shard_map.46 = f32[4,2,12,588]{3,2,1,0:T(8,128)S(1)} custom-call(bf16[4,2,5,192,192]{4,3,2,1,0:T(8,128)(2,1)} %a_ref.1, s32[4,2,5]{2,1,0:T(2,128)} %a_codes.1, bf16[4,3,12,2,192]{4,3,2,1,0:T(2,128)(2,1)} %bitcast.2, s32[3,2,4]{2,1,0:T(2,128)} %bitcast.3), custom_call_target="tpu_custom_call" | custom-call | tf_op jit(solution)/shard_map/pallas_call | solution.py:364
  30.6 0.8 %copy.5 = f32[4,2,12,588]{3,1,2,0:T(2,128)} copy(f32[4,2,12,588]{3,2,1,0:T(8,128)S(1)} %shard_map.46) | data formatting | bytes 451584 | tf_op jit(solution)/shard_map/pallas_call | solution.py:364

commit v5 on v4

--- a/solution.py
+++ b/solution.py
@@ -84,8 +84,8 @@
 
 def kernel(
     a_ref, a_codes, p_ref, p_codes, out_ref,
-    a_buf, p_buf, mid, inner_side, outer_side, packed, got, rows_w, own, send_y, got_y, send_x, got_x,
-    a_sem, p_sem, side_out, side_in, mid_out, mid_in, y_out, y_in, x_out, x_in, ready,
+    a_buf, p_buf, mid, inner_side, outer_side, packed, got, half, half_sent, half_got, rows_w, turned_w, own, send_y, got_y, send_x, got_x,
+    a_sem, p_sem, side_out, side_in, mid_out, mid_in, y_out, y_in, x_out, x_in, half_out, half_in, ready,
 ):
     tile_x, tile_y, slots_a, edges, _ = a_ref.shape
     slots_p, unknowns = p_ref.shape[1], p_ref.shape[2]
@@ -126,7 +126,7 @@
     def a_copy(x, y):
         return pltpu.make_async_copy(a_ref.at[x, y], a_buf.at[x, y], a_sem.at[x, y])
 
-    for y in (inner, outer):
+    for y in (outer, inner):
         for x in range(tile_x):
             a_copy(x, y).start()
 
@@ -147,8 +147,12 @@
                 holds[columns] = jnp.zeros_like(holds[columns])
                 if step_x == 0:
                     got_y[side] = jnp.zeros(got_y.shape[1:], got_y.dtype)
+                    if side:
+                        half_got[...] = jnp.zeros_like(half_got)
 
     rows_w[:, :, :, :, edges:] = jnp.zeros((tile_x, tile_y, slots_a, 2 * span, WIDE - edges), jnp.bfloat16)
+    turned_w[:, :, :, edges:] = jnp.zeros((tile_x, 3, 2 * span, WIDE - edges), jnp.bfloat16)
+    half[:, :, edges:] = jnp.zeros((tile_x, span, WIDE - edges), jnp.bfloat16)
 
     pl.when(earlier_ones > 0)(lambda: pl.semaphore_wait(barrier, earlier_ones))
     for step_x, step_y in WAYS:
@@ -225,20 +229,63 @@
             device_id_type=pl.DeviceIdType.MESH,
         )
 
+    def half_copy():
+        return pltpu.make_async_remote_copy(
+            src_ref=half_sent,
+            dst_ref=half_got,
+            send_sem=half_out,
+            recv_sem=half_in,
+            device_id=(at_x, at_y + 2 * outer - 1),
+            device_id_type=pl.DeviceIdType.MESH,
+        )
+
     def when_inside(step_x, step_y, does):
         pl.when(inside(step_x, step_y))(does)
 
-    def first(y):
+    def first(side):
+        y = rows[side]
         for x in range(tile_x):
             a_copy(x, y).wait()
             here = mid[y, x + 1, :, :edges]
+            outward = [jnp.zeros((2 * span, edges), jnp.bfloat16)] * 3
             for k in range(slots_a):
                 product = jnp.dot(here, a_buf[x, y, k], preferred_element_type=jnp.float32)
                 high = product.astype(jnp.bfloat16)
-                rows_w[x, y, k, :span, :edges] = high
-                rows_w[x, y, k, span:, :edges] = (product - high.astype(jnp.float32)).astype(jnp.bfloat16)
+                low = (product - high.astype(jnp.float32)).astype(jnp.bfloat16)
+                both = jnp.concatenate([high, low], axis=0)
+                rows_w[x, y, k, :, :edges] = both
+                if side:
+                    code = a_codes[x, y, k]
+                    outward = [jnp.where(code == 3 * i + 2 * y, both, value) for i, value in enumerate(outward)]
+            if side:
+                for i, value in enumerate(outward):
+                    turned_w[x, i, :, :edges] = value
+                    leaves = jnp.zeros((SLOT, edges), jnp.bfloat16)
+                    for m in range(1, slots_p):
+                        leaves = jnp.where(p_codes[m, y, x] == y + 3, value[SLOT * m : SLOT * (m + 1)], leaves)
+                    half[x, SLOT * i : SLOT * (i + 1), :edges] = leaves
+                half_sent[x] = pack(half[x], slots_p, unknowns)
 
     lane = lax.broadcasted_iota(jnp.int32, (span, COLS), 1).astype(jnp.float32)
+
+    def placed(block, there, base):
+        target = there[:, edges : edges + 1].astype(jnp.float32) + base
+        chosen = jnp.where(lane == target, 1.0, 0.0).astype(jnp.bfloat16)
+        return jnp.dot(block.astype(jnp.bfloat16), chosen, preferred_element_type=jnp.float32)
+
+    def across(left, there):
+        return lax.dot_general(left, there, (((1,), (1,)), ((), ())), preferred_element_type=jnp.float32)
+
+    def store(x, y, summed, add):
+        def put_own(q, value):
+            own[q, x, y] = own[q, x, y] + value if add else value
+
+        put_own(0, summed[:SLOT])
+        for q in range(1, 5):
+            value = jnp.zeros((SLOT, COLS), jnp.float32)
+            for m in range(1, slots_p):
+                value += jnp.where(p_codes[m, y, x] == q, summed[SLOT * m : SLOT * (m + 1)], 0.0)
+            put_own(q, value)
 
     def second(side):
         y = rows[side]
@@ -249,31 +296,46 @@
                 live = code < 9
                 code = jnp.where(live, code, 4)
                 step_x, step_y = code // 3 - 1, code % 3 - 1
-                there = jnp.where(
-                    step_y == 2 * y - 1,
-                    sides[side][x + 1 + step_x],
-                    mid[jnp.clip(y + step_y, 0, tile_y - 1), x + 1 + step_x],
-                )
+                away = step_y == 2 * y - 1
+                there = mid[jnp.clip(y + step_y, 0, tile_y - 1), x + 1 + step_x]
+                if side:
+                    live = live & jnp.logical_not(away)
+                else:
+                    there = jnp.where(away, inner_side[x + 1 + step_x], there)
                 base = jnp.where(live, unknowns * (5 * (step_x + 2) + step_y + 2), -4096).astype(jnp.float32)
-                both = lax.dot_general(
-                    rows_w[x, y, k], there, (((1,), (1,)), ((), ())), preferred_element_type=jnp.float32
-                )
-                block = (both[:span] + both[span:]).astype(jnp.bfloat16)
-                target = there[:, edges : edges + 1].astype(jnp.float32) + base
-                chosen = jnp.where(lane == target, 1.0, 0.0).astype(jnp.bfloat16)
-                summed += jnp.dot(block, chosen, preferred_element_type=jnp.float32)
-            own[0, x, y] = summed[:SLOT]
-            for q in range(1, 5):
-                value = jnp.zeros((SLOT, COLS), jnp.float32)
-                for m in range(1, slots_p):
-                    value += jnp.where(p_codes[m, y, x] == q, summed[SLOT * m : SLOT * (m + 1)], 0.0)
-                own[q, x, y] = value
-
-    def send_contributions(side):
+                both = across(rows_w[x, y, k], there)
+                summed += placed(both[:span] + both[span:], there, base)
+            store(x, y, summed, False)
+
+    def second_outward():
+        for x in range(tile_x):
+            summed = jnp.zeros((span, COLS), jnp.float32)
+            for i in range(3):
+                there = outer_side[x + i]
+                base = (unknowns * (5 * (i + 1) + 2 * outer + 1)).astype(jnp.float32)
+                both = across(turned_w[x, i], there)
+                summed += placed(both[:span] + both[span:], there, base)
+            store(x, outer, summed, True)
+
+    def second_inward(x):
+        high, rest = unpack(half_got[x], slots_p, unknowns)
+        rest = jnp.where(lax.broadcasted_iota(jnp.int32, rest.shape, 1) < edges - 128, rest, jnp.zeros_like(rest))
+        left = jnp.concatenate([high, rest], axis=1)
+        summed = jnp.zeros((SLOT, COLS), jnp.float32)
+        for i in range(3):
+            there = mid[outer, x + i]
+            product = across(left[SLOT * i : SLOT * (i + 1)], there)
+            summed += placed(product, there, float(unknowns * (5 * (i + 1) + 2)))
+        return summed
+
+    def send_y_contributions(side):
         y = rows[side]
         for x in range(tile_x):
             send_y[side, x] = own[y + 3, x, y].astype(jnp.bfloat16)
         when_inside(0, 2 * y - 1, lambda: y_copy(side).start())
+
+    def send_x_contributions(side):
+        y = rows[side]
         for way in range(2):
             send_x[way, side] = own[way + 1, (tile_x - 1) * way, y].astype(jnp.bfloat16)
             when_inside(2 * way - 1, 0, lambda: x_copy(way, side).start())
@@ -292,22 +354,19 @@
             pl.semaphore_wait(ready.at[(step_x + 1) * 3 + step_y + 1], 1)
             copy().start()
 
-    def both_firsts(i, _):
-        first(jnp.where(i == 0, inner, outer))
-        return 0
-
-    lax.fori_loop(0, 2, both_firsts, 0)
-
+    first(1)
+    when_inside(0, 2 * outer - 1, lambda: half_copy().start())
     for way in range(2):
         when_inside(1 - 2 * way, 0, lambda: mid_copy(way).wait_recv())
-    for side in range(2):
-        for step_x in (0, -1, 1):
-            when_inside(-step_x, 2 * rows[side] - 1, lambda: side_copy(step_x, side).wait_recv())
-        if side:
-            for x in range(tile_x + 2):
-                outer_side[x, :, :128], outer_side[x, :, 128:] = unpack(got[x], slots_p, unknowns)
-        second(side)
-        send_contributions(side)
+    second(1)
+    send_y_contributions(1)
+
+    first(0)
+    for step_x in (0, -1, 1):
+        when_inside(-step_x, 2 * inner - 1, lambda: side_copy(step_x, 0).wait_recv())
+    second(0)
+    send_y_contributions(0)
+    send_x_contributions(0)
 
     def put(x, y, pieces, add):
         total = None
@@ -321,6 +380,13 @@
                 tile = tile + out_ref[x, y, :, 128 * j : high]
             out_ref[x, y, :, 128 * j : high] = tile
 
+    for step_x in (0, -1, 1):
+        when_inside(-step_x, 2 * outer - 1, lambda: side_copy(step_x, 1).wait_recv())
+    for x in range(tile_x + 2):
+        outer_side[x, :, :128], outer_side[x, :, 128:] = unpack(got[x], slots_p, unknowns)
+    second_outward()
+    send_x_contributions(1)
+
     for x in range(tile_x):
         for y in range(tile_y):
             pieces = []
@@ -329,6 +395,10 @@
                 if 0 <= from_x < tile_x and 0 <= from_y < tile_y:
                     pieces.append((own[face, from_x, from_y], face))
             put(x, y, pieces, False)
+
+    when_inside(0, 2 * outer - 1, lambda: half_copy().wait_recv())
+    for x in range(tile_x):
+        put(x, outer, [(second_inward(x), 0)], True)
 
     for way in range(2):
         for side in range(2):
@@ -354,6 +424,7 @@
             when_inside(2 * way - 1, 0, lambda: x_copy(way, side).wait_send())
     for way in range(2):
         when_inside(2 * way - 1, 0, lambda: mid_copy(way).wait_send())
+    when_inside(0, 2 * outer - 1, lambda: half_copy().wait_send())
 
 
 def shards(a_blocks, a_codes, p_blocks, p_codes):
@@ -379,7 +450,11 @@
             pltpu.VMEM((tile_x + 2, span, WIDE), jnp.bfloat16),
             pltpu.VMEM((tile_x, PACK, 128), jnp.bfloat16),
             pltpu.VMEM((tile_x + 2, PACK, 128), jnp.bfloat16),
+            pltpu.VMEM((tile_x, span, WIDE), jnp.bfloat16),
+            pltpu.VMEM((tile_x, PACK, 128), jnp.bfloat16),
+            pltpu.VMEM((tile_x, PACK, 128), jnp.bfloat16),
             pltpu.VMEM((tile_x, tile_y, slots_a, 2 * span, WIDE), jnp.bfloat16),
+            pltpu.VMEM((tile_x, 3, 2 * span, WIDE), jnp.bfloat16),
             pltpu.VMEM((5, tile_x, tile_y, SLOT, COLS), jnp.float32),
             pltpu.VMEM((tile_y, tile_x, SLOT, COLS), jnp.bfloat16),
             pltpu.VMEM((tile_y, tile_x, SLOT, COLS), jnp.bfloat16),
@@ -395,6 +470,8 @@
             dma((2,)),
             dma((2, 2)),
             dma((2, 2)),
+            dma,
+            dma,
             pltpu.SemaphoreType.REGULAR((9,)),
         ],
         compiler_params=pltpu.CompilerParams(

time: 31.6 us -> 26.6 us (0.84)
  the two profiles are of different devices: /device:TPU:34 before, /device:TPU:30 now
where the time goes in v5:
time: 26.6 us; the launch traced here: 26.4 us
  Pallas kernels  25.6 us (96%)
  local copies, waits for them, and re-layouts  0.82 us (3%)
    pallas_call x1, Pallas kernels, shards(): pl.pallas_call(kernel, out_shape=jax.ShapeDtypeStruct((tile_x, tile_y, un...  25.6 us
    pallas_call x1, local copies, waits for them, and re-layouts, shards(): pl.pallas_call(kernel, out_shape=jax.ShapeDtypeStruct((tile_x, tile_y, un...  0.82 us

profile of v5, /device:TPU:30, one launch (start us, length us, event | category | flops | bytes accessed | tf_op | source)
XLA Modules:
  0.0 26.4 jit_solution(9956595248721636452)
XLA Ops:
  0.0 25.6 %shard_map.46 = f32[4,2,12,588]{3,2,1,0:T(8,128)S(1)} custom-call(bf16[4,2,5,192,192]{4,3,2,1,0:T(8,128)(2,1)} %a_ref.1, s32[4,2,5]{2,1,0:T(2,128)} %a_codes.1, bf16[4,3,12,2,192]{4,3,2,1,0:T(2,128)(2,1)} %bitcast.2, s32[3,2,4]{2,1,0:T(2,128)} %bitcast.3), custom_call_target="tpu_custom_call" | custom-call | tf_op jit(solution)/shard_map/pallas_call | solution.py:435
  25.6 0.8 %copy.5 = f32[4,2,12,588]{3,1,2,0:T(2,128)} copy(f32[4,2,12,588]{3,2,1,0:T(8,128)S(1)} %shard_map.46) | data formatting | bytes 451584 | tf_op jit(solution)/shard_map/pallas_call | solution.py:435

commit v6 on v5

--- a/solution.py
+++ b/solution.py
@@ -84,7 +84,7 @@
 
 def kernel(
     a_ref, a_codes, p_ref, p_codes, out_ref,
-    a_buf, p_buf, mid, inner_side, outer_side, packed, got, half, half_sent, half_got, rows_w, turned_w, own, send_y, got_y, send_x, got_x,
+    a_buf, p_buf, mid, inner_side, outer_side, packed, got, half, half_sent, half_got, rows_w, own, send_y, got_y, send_x, got_x,
     a_sem, p_sem, side_out, side_in, mid_out, mid_in, y_out, y_in, x_out, x_in, half_out, half_in, ready,
 ):
     tile_x, tile_y, slots_a, edges, _ = a_ref.shape
@@ -151,41 +151,51 @@
                         half_got[...] = jnp.zeros_like(half_got)
 
     rows_w[:, :, :, :, edges:] = jnp.zeros((tile_x, tile_y, slots_a, 2 * span, WIDE - edges), jnp.bfloat16)
-    turned_w[:, :, :, edges:] = jnp.zeros((tile_x, 3, 2 * span, WIDE - edges), jnp.bfloat16)
-    half[:, :, edges:] = jnp.zeros((tile_x, span, WIDE - edges), jnp.bfloat16)
-
-    pl.when(earlier_ones > 0)(lambda: pl.semaphore_wait(barrier, earlier_ones))
-    for step_x, step_y in WAYS:
-        @pl.when(inside(step_x, step_y) & jnp.logical_not(later(step_x, step_y)))
-        def _():
-            pl.semaphore_signal(
-                ready.at[(1 - step_x) * 3 + 1 - step_y],
-                inc=1,
-                device_id=(at_x + step_x, at_y + step_y),
-                device_id_type=pl.DeviceIdType.MESH,
-            )
-
-    p_copy.wait()
-    taken = slots_p * unknowns * tile_y
-    target_row = lax.broadcasted_iota(jnp.int32, (tile_y * span, taken), 0)
-    source_row = lax.broadcasted_iota(jnp.int32, (tile_y * span, taken), 1)
-    row = lax.broadcasted_iota(jnp.int32, (span, WIDE - edges), 0)
-    for x in range(tile_x):
-        wanted = jnp.full_like(target_row, -1)
-        for y in range(tile_y):
-            place = row % SLOT
-            for m in range(slots_p):
-                code = p_codes[m, y, x]
-                first_row = y * span + m * SLOT
-                fits = (target_row >= first_row) & (target_row < first_row + unknowns) & (code < 5)
-                wanted = jnp.where(fits, (target_row - first_row + m * unknowns) * tile_y + y, wanted)
-                shift = jnp.where(code == 1, -5, jnp.where(code == 2, 5, jnp.where(code == 3, -1, jnp.where(code == 4, 1, 0))))
-                place = place + jnp.where(row // SLOT == m, shift * unknowns, 0)
-            mid[y, x + 1, :, edges:] = place.astype(jnp.float32).astype(jnp.bfloat16)
-        order = jnp.where(wanted == source_row, 1.0, 0.0).astype(jnp.bfloat16)
-        laid = jnp.dot(order, p_buf[x].reshape(taken, edges), preferred_element_type=jnp.float32).astype(jnp.bfloat16)
-        for y in range(tile_y):
-            mid[y, x + 1, :, :edges] = laid[y * span : (y + 1) * span]
+
+    def greet():
+        pl.when(earlier_ones > 0)(lambda: pl.semaphore_wait(barrier, earlier_ones))
+        for step_x, step_y in WAYS:
+            @pl.when(inside(step_x, step_y) & jnp.logical_not(later(step_x, step_y)))
+            def _():
+                pl.semaphore_signal(
+                    ready.at[(1 - step_x) * 3 + 1 - step_y],
+                    inc=1,
+                    device_id=(at_x + step_x, at_y + step_y),
+                    device_id_type=pl.DeviceIdType.MESH,
+                )
+
+    def lay_out():
+        p_copy.wait()
+        taken = slots_p * unknowns * tile_y
+        target_row = lax.broadcasted_iota(jnp.int32, (tile_y * span, taken), 0)
+        source_row = lax.broadcasted_iota(jnp.int32, (tile_y * span, taken), 1)
+        row = lax.broadcasted_iota(jnp.int32, (span, WIDE - edges), 0)
+        for x in range(tile_x):
+            wanted = jnp.full_like(target_row, -1)
+            for y in range(tile_y):
+                place = row % SLOT
+                for m in range(slots_p):
+                    code = p_codes[m, y, x]
+                    first_row = y * span + m * SLOT
+                    fits = (target_row >= first_row) & (target_row < first_row + unknowns) & (code < 5)
+                    wanted = jnp.where(fits, (target_row - first_row + m * unknowns) * tile_y + y, wanted)
+                    shift = jnp.where(code == 1, -5, jnp.where(code == 2, 5, jnp.where(code == 3, -1, jnp.where(code == 4, 1, 0))))
+                    place = place + jnp.where(row // SLOT == m, shift * unknowns, 0)
+                mid[y, x + 1, :, edges:] = place.astype(jnp.float32).astype(jnp.bfloat16)
+            order = jnp.where(wanted == source_row, 1.0, 0.0).astype(jnp.bfloat16)
+            laid = jnp.dot(order, p_buf[x].reshape(taken, edges), preferred_element_type=jnp.float32).astype(jnp.bfloat16)
+            for y in range(tile_y):
+                mid[y, x + 1, :, :edges] = laid[y * span : (y + 1) * span]
+
+    steps = start_order(at_x, at_y) // 1024 - start_order(at_x, at_y + 2 * outer - 1) // 1024
+    turn = jnp.where((steps >= 0) & (steps <= 3), 1, 0)
+
+    def start_up(i, _):
+        pl.when(i == turn)(greet)
+        pl.when(i != turn)(lay_out)
+        return 0
+
+    lax.fori_loop(0, 2, start_up, 0)
 
     def side_copy(step_x, side):
         source = {0: pl.ds(1, tile_x), -1: pl.ds(1, 1), 1: pl.ds(tile_x, 1)}[step_x]
@@ -242,28 +252,32 @@
     def when_inside(step_x, step_y, does):
         pl.when(inside(step_x, step_y))(does)
 
+    def outward_slot(x, i):
+        slot, found = jnp.int32(0), False
+        for k in range(slots_a):
+            fits = a_codes[x, outer, k] == 3 * i + 2 * outer
+            slot, found = jnp.where(fits, k, slot), found | fits
+        return slot, found
+
     def first(side):
         y = rows[side]
         for x in range(tile_x):
             a_copy(x, y).wait()
             here = mid[y, x + 1, :, :edges]
-            outward = [jnp.zeros((2 * span, edges), jnp.bfloat16)] * 3
             for k in range(slots_a):
                 product = jnp.dot(here, a_buf[x, y, k], preferred_element_type=jnp.float32)
                 high = product.astype(jnp.bfloat16)
                 low = (product - high.astype(jnp.float32)).astype(jnp.bfloat16)
-                both = jnp.concatenate([high, low], axis=0)
-                rows_w[x, y, k, :, :edges] = both
-                if side:
-                    code = a_codes[x, y, k]
-                    outward = [jnp.where(code == 3 * i + 2 * y, both, value) for i, value in enumerate(outward)]
+                rows_w[x, y, k, :span, :edges] = high
+                rows_w[x, y, k, span:, :edges] = low
             if side:
-                for i, value in enumerate(outward):
-                    turned_w[x, i, :, :edges] = value
-                    leaves = jnp.zeros((SLOT, edges), jnp.bfloat16)
+                for i in range(3):
+                    slot, found = outward_slot(x, i)
+                    leaves = jnp.zeros((SLOT, WIDE), jnp.bfloat16)
                     for m in range(1, slots_p):
-                        leaves = jnp.where(p_codes[m, y, x] == y + 3, value[SLOT * m : SLOT * (m + 1)], leaves)
-                    half[x, SLOT * i : SLOT * (i + 1), :edges] = leaves
+                        block = rows_w[x, y, slot, SLOT * m : SLOT * (m + 1)]
+                        leaves = jnp.where(found & (p_codes[m, y, x] == y + 3), block, leaves)
+                    half[x, SLOT * i : SLOT * (i + 1)] = leaves
                 half_sent[x] = pack(half[x], slots_p, unknowns)
 
     lane = lax.broadcasted_iota(jnp.int32, (span, COLS), 1).astype(jnp.float32)
@@ -312,8 +326,9 @@
             summed = jnp.zeros((span, COLS), jnp.float32)
             for i in range(3):
                 there = outer_side[x + i]
-                base = (unknowns * (5 * (i + 1) + 2 * outer + 1)).astype(jnp.float32)
-                both = across(turned_w[x, i], there)
+                slot, found = outward_slot(x, i)
+                base = jnp.where(found, unknowns * (5 * (i + 1) + 2 * outer + 1), -4096).astype(jnp.float32)
+                both = across(rows_w[x, outer, slot], there)
                 summed += placed(both[:span] + both[span:], there, base)
             store(x, outer, summed, True)
 
@@ -454,7 +469,6 @@
             pltpu.VMEM((tile_x, PACK, 128), jnp.bfloat16),
             pltpu.VMEM((tile_x, PACK, 128), jnp.bfloat16),
             pltpu.VMEM((tile_x, tile_y, slots_a, 2 * span, WIDE), jnp.bfloat16),
-            pltpu.VMEM((tile_x, 3, 2 * span, WIDE), jnp.bfloat16),
             pltpu.VMEM((5, tile_x, tile_y, SLOT, COLS), jnp.float32),
             pltpu.VMEM((tile_y, tile_x, SLOT, COLS), jnp.bfloat16),
             pltpu.VMEM((tile_y, tile_x, SLOT, COLS), jnp.bfloat16),

time: 26.6 us -> 26.6 us (level)
  the two profiles are of different devices: /device:TPU:30 before, /device:TPU:102 now
where the time goes in v6:
time: 26.6 us; the launch traced here: 26.5 us
  Pallas kernels  25.6 us (96%)
  local copies, waits for them, and re-layouts  0.82 us (3%)
    pallas_call x1, Pallas kernels, shards(): pl.pallas_call(kernel, out_shape=jax.ShapeDtypeStruct((tile_x, tile_y, un...  25.6 us
    pallas_call x1, local copies, waits for them, and re-layouts, shards(): pl.pallas_call(kernel, out_shape=jax.ShapeDtypeStruct((tile_x, tile_y, un...  0.82 us

profile of v6, /device:TPU:102, one launch (start us, length us, event | category | flops | bytes accessed | tf_op | source)
XLA Modules:
  0.0 26.5 jit_solution(18433720558882784295)
XLA Ops:
  0.0 25.6 %shard_map.46 = f32[4,2,12,588]{3,2,1,0:T(8,128)S(1)} custom-call(bf16[4,2,5,192,192]{4,3,2,1,0:T(8,128)(2,1)} %a_ref.1, s32[4,2,5]{2,1,0:T(2,128)} %a_codes.1, bf16[4,3,12,2,192]{4,3,2,1,0:T(2,128)(2,1)} %bitcast.2, s32[3,2,4]{2,1,0:T(2,128)} %bitcast.3), custom_call_target="tpu_custom_call" | custom-call | tf_op jit(solution)/shard_map/pallas_call | solution.py:450
  25.6 0.8 %copy.5 = f32[4,2,12,588]{3,1,2,0:T(2,128)} copy(f32[4,2,12,588]{3,2,1,0:T(8,128)S(1)} %shard_map.46) | data formatting | bytes 451584 | tf_op jit(solution)/shard_map/pallas_call | solution.py:450
